TPU v7x, 32 devices: a whole 2x2x4 slice. The times are simulated.
32 devices in a mesh: seq: 8 (over z, y), head: 4 (over x, core).
Axes of the slice: x: 2, y: 2, z: 4, core: 2. Of those that a mesh axis runs over, the one named last changes fastest.
Arguments:
- query: bfloat16 [384, 1536], P('seq', 'head'), may hold values from -64 to 64
- new_kv: bfloat16 [2, 384, 1536], P(None, 'seq', 'head'), may hold values from -6 to 6
- cache_kv: bfloat16 [2, 1024, 1536], P(None, 'seq', 'head'), may hold values from -6 to 6
- text_kv: bfloat16 [2, 512, 1536], P(None, None, 'head'), may hold values from -8 to 8
- active: int32 [384], P('seq'), may hold values from 0 to 1023, as said below
- counts: int32 [8], P('seq'), may hold values from 0 to 48, as said below
- hidden: bfloat16 [384, 3072], P('seq', 'head'), may hold values from -64 to 64
- w_out: bfloat16 [1536, 3072], P('head'), may hold values from -0.4375 to 0.4375
- mod_shift: float32 [3072], P('head'), may hold values from -3 to 3
- mod_scale: float32 [3072], P('head'), may hold values from -3 to 3
- w_final: float32 [3072, 64], P('head'), may hold values from -0.109375 to 0.109375
- latent: float32 [1024, 64], P('seq'), may hold values from -6 to 6
- cached_velocity: float32 [1024, 64], P('seq'), may hold values from -6 to 6
- step_size: float32 [1], replicated, may hold values from -0.6 to -0.1
Outputs:
- velocity: float32 [1024, 64], P('seq')
- latent_next: float32 [1024, 64], P('seq')
Inputs may be any that keep to these rules, and one draw needn't show every extreme that they name: `active`: for shard k, the entries k * 48 to k * 48 + counts[k] - 1 are distinct image tokens of that shard (k * 128 to (k + 1) * 128 - 1); the later entries of the shard are tokens of the same shard and carry no meaning. The counts sum to exactly 24 times the number of shards; some shard has 48 and some shard has 0.
All inputs are finite; a program needn't handle non-finite values.
Results may differ from a plain program's by a relative error of at most 0.0035.
Values may be sent and summed in bfloat16 or wider, within the bound.
A program may use at most 128 MiB of HBM per device.

v0:
```python
import jax
import jax.numpy as jnp
from jax import lax
from jax.sharding import PartitionSpec as P

D = 3072
HD = 128


EPS = 1e-06


def block_rows(row_count):
    for pieces in range(1, row_count + 1):
        if row_count % pieces == 0 and row_count // pieces <= 512:
            return row_count // pieces
    return row_count


def partial_attention(queries, keys, values):
    row_count, row_width = queries.shape
    head_count = row_width // HD
    block = block_rows(row_count)
    keys_split = keys.reshape(keys.shape[0], head_count, HD)
    values_split = values.reshape(values.shape[0], head_count, HD)

    def one_block(rows_in):
        split = rows_in.reshape(block, head_count, HD)
        scores = jnp.einsum(
            "qhd,khd->hqk", split, keys_split, preferred_element_type=jnp.float32
        ) * HD ** (-0.5)
        row_max = jnp.max(scores, axis=2, keepdims=True)
        weights = jnp.exp(scores - row_max)
        weight_sum = jnp.sum(weights, axis=2)
        numerator = jnp.einsum(
            "hqk,khd->qhd",
            weights.astype(jnp.bfloat16),
            values_split,
            preferred_element_type=jnp.float32,
        )
        blended = numerator / jnp.transpose(weight_sum)[:, :, None]
        spread = jnp.transpose(row_max[:, :, 0] + jnp.log(weight_sum))
        return (blended.reshape(block, row_width), spread)

    blended, spread = lax.map(one_block, queries.reshape(row_count // block, block, row_width))
    return (blended.reshape(row_count, row_width), spread.reshape(row_count, head_count))


def merge_pair(first, second):
    blend_a, spread_a = first
    blend_b, spread_b = second
    joint = jnp.logaddexp(spread_a, spread_b)
    row_count, row_width = blend_a.shape
    head_count = spread_a.shape[1]
    share_a = jnp.exp(spread_a - joint)[:, :, None]
    share_b = jnp.exp(spread_b - joint)[:, :, None]
    merged = (
        blend_a.reshape(row_count, head_count, HD) * share_a
        + blend_b.reshape(row_count, head_count, HD) * share_b
    )
    return (merged.reshape(row_count, row_width), joint)


def merge_sources(pieces):
    blended, spread = pieces
    sources, row_count, row_width = blended.shape
    head_count = spread.shape[2]
    joint = jax.nn.logsumexp(spread, axis=0)
    shares = jnp.exp(spread - joint[None])
    merged = jnp.sum(
        blended.reshape(sources, row_count, head_count, HD) * shares[..., None], axis=0
    )
    return (merged.reshape(row_count, row_width), joint)


def on_device(
    query,
    new_kv,
    cache_kv,
    text_kv,
    active,
    counts,
    hidden,
    w_out,
    mod_shift,
    mod_scale,
    w_final,
    latent,
    cached_velocity,
    step_size,
):
    shards = lax.axis_size("seq")
    own_index = lax.axis_index("seq")
    slot_count, row_width = query.shape
    head_count = row_width // HD
    tok_rows = cache_kv.shape[1]
    live_slots = jnp.arange(slot_count, dtype=jnp.int32) < counts[0]
    local_pos = active - own_index * tok_rows
    matched = (local_pos[None, :] == jnp.arange(tok_rows, dtype=jnp.int32)[:, None]) & live_slots[
        None, :
    ]
    replaced = jnp.any(matched, axis=1)
    placed = jnp.einsum(
        "tc,scw->stw", matched.astype(jnp.bfloat16), new_kv, preferred_element_type=jnp.float32
    ).astype(jnp.bfloat16)
    image_kv = jnp.where(replaced[None, :, None], placed, cache_kv)
    gathered = lax.all_gather(query, "seq", axis=0, tiled=True)
    blended, spread = partial_attention(gathered, image_kv[0], image_kv[1])
    blended, spread = merge_sources(
        (
            lax.all_to_all(
                blended.reshape(shards, slot_count, row_width),
                "seq",
                split_axis=0,
                concat_axis=0,
                tiled=True,
            ),
            lax.all_to_all(
                spread.reshape(shards, slot_count, head_count),
                "seq",
                split_axis=0,
                concat_axis=0,
                tiled=True,
            ),
        )
    )
    text_blend, text_spread = partial_attention(query, text_kv[0], text_kv[1])
    blended, spread = merge_pair((blended, spread), (text_blend, text_spread))
    attended = blended.astype(jnp.bfloat16)
    col_terms = jnp.dot(attended, w_out, preferred_element_type=jnp.float32)
    projected = lax.psum_scatter(
        col_terms.astype(jnp.bfloat16), "head", scatter_dimension=1, tiled=True
    ).astype(jnp.float32)
    residual_sum = hidden.astype(jnp.float32) + projected
    lifted = 1.0 + mod_scale
    row_sums = jnp.sum(residual_sum, axis=1)
    row_squares = jnp.sum(residual_sum * residual_sum, axis=1)
    scaled_part = jnp.dot(residual_sum * lifted, w_final, precision=lax.Precision.HIGHEST)
    column_part = jnp.dot(lifted[None, :], w_final, precision=lax.Precision.HIGHEST)
    offset_part = jnp.dot(mod_shift[None, :], w_final, precision=lax.Precision.HIGHEST)
    scaled_part, column_part, offset_part, row_sums, row_squares = lax.psum(
        (scaled_part, column_part, offset_part, row_sums, row_squares), "head"
    )
    row_mean = row_sums / D
    inverse = lax.rsqrt(row_squares / D - row_mean * row_mean + EPS)
    fresh = (scaled_part - row_mean[:, None] * column_part) * inverse[:, None] + offset_part
    chosen = jnp.dot(matched.astype(jnp.float32), fresh, precision=lax.Precision.HIGHEST)
    velocity = jnp.where(replaced[:, None], chosen, cached_velocity)
    latent_next = latent + step_size[0] * velocity
    return (velocity, latent_next)


def solution(mesh):
    in_specs = (
        P("seq", "head"),
        P(None, "seq", "head"),
        P(None, "seq", "head"),
        P(None, None, "head"),
        P("seq"),
        P("seq"),
        P("seq", "head"),
        P("head", None),
        P("head"),
        P("head"),
        P("head", None),
        P("seq", None),
        P("seq", None),
        P(),
    )
    out_specs = (P("seq", None), P("seq", None))
    return jax.shard_map(
        on_device, mesh=mesh, in_specs=in_specs, out_specs=out_specs, check_vma=False
    )
```

profile of v0, /device:TPU:0, one launch (start us, length us, event | category | flops | bytes accessed | tf_op | source)
XLA Modules:
  0.0 119.9 jit_solution(14968936652232083363)
XLA Ops:
  8.8 1.3 %fusion.3 = bf16[2,128,384]{2,1,0:T(8,128)(2,1)S(1)} fusion(bf16[2,128,384]{2,1,0:T(8,128)(2,1)} %param.16, bf16[2,48,384]{2,1,0:T(8,128)(2,1)} %param.15, pred[128]{0:T(512)(128)(4,1)S(1)} %fusion.31, s32[48]{0:T(128)S(1)} %broadcast_subtract_fusion, pred[48]{0:T(512)(128)(4,1)S(1)} %iota_compare_fusion.1), kind=kOutput, calls=%fused_computation.8 | convolution fusion | flops 9646080 | bytes 467312 | tf_op jit(solution)/shard_map/tc,scw->stw/dot_general | solution.py:103
  10.2 32.8 %all_gather.3 = bf16[384,384]{1,0:T(8,128)(2,1)S(1)} all-gather(bf16[48,384]{1,0:T(8,128)(2,1)} %param.14), channel_id=1, replica_groups=mesh['seq'=8,'head'=4] {'seq'}, dimensions={0}, use_global_device_ids=true | all-gather | bytes 331776 | tf_op jit(solution)/shard_map/all_gather | solution.py:107
  44.5 5.6 %all-to-all-start.1 = ((f32[8,1,144]{2,1,0:T(1,128)}), f32[8,1,144]{2,1,0:T(1,128)}, u32[]{:S(2)}, u32[]{:S(2)}) async-start(f32[8,1,144]{2,1,0:T(1,128)} %reshape.86), calls=%async_computation.1 | async-start | bytes 16384 | tf_op jit(solution)/shard_map/all_to_all | solution.py:118
  50.1 0.7 copy.119
  50.8 2.1 %fusion.41 = (bf16[1,512,384]{2,1,0:T(8,128)(2,1)}, bf16[1,512,384]{2,1,0:T(8,128)(2,1)}) fusion(bf16[2,512,384]{2,1,0:T(8,128)(2,1)} %param.17), kind=kLoop, calls=%fused_computation.68 | loop fusion | bytes 1572864 | tf_op jit(solution)/shard_map/slice | solution.py:127
  52.9 1.2 copy.147
  54.4 2.1 %fusion = f32[384,3,128]{0,2,1:T(8,128)} fusion(bf16[128,3,128]{0,2,1:T(8,128)(2,1)} %bitcast.95, f32[3,384,128]{1,2,0:T(8,128)S(1)} %get-tuple-element.54, f32[384,3]{0,1:T(4,128)} %bitcast.97, f32[3,384]{1,0:T(4,128)S(1)} %get-tuple-element.53), kind=kOutput, calls=%fused_computation.3 | convolution fusion | flops 38191104 | bytes 1287168 | tf_op jit(solution)/shard_map/while/body/eval_jaxpr/hqk,khd->qhd/dot_general | solution.py:35
  56.6 1.4 %copy.125 = f32[384,3,128]{2,1,0:T(4,128)S(1)} copy(f32[384,3,128]{0,2,1:T(8,128)} %fusion) | data formatting | bytes 1179648 | tf_op jit(solution)/shard_map/while/body/eval_jaxpr/div | solution.py:41
  58.0 1.1 reshape_reshape.7
  59.1 0.9 copy.148
  60.1 6.1 %all-to-all-start = ((f32[8,48,384]{2,1,0:T(8,128)}), f32[8,48,384]{2,1,0:T(8,128)}, u32[]{:S(2)}, u32[]{:S(2)}) async-start(f32[8,48,384]{2,1,0:T(8,128)} %reshape_reshape.7), calls=%async_computation | async-start | bytes 1179648 | tf_op jit(solution)/shard_map/all_to_all | solution.py:111
  66.8 1.4 %reduce.1 = f32[8,144]{1,0:T(8,128)S(1)} reduce(f32[8,1,144]{2,1,0:T(1,128)} %all-to-all-done.1, f32[]{:T(128)} %broadcast.51), dimensions={1}, to_apply=%all_to_all.7.reduce_sub_computation | reduce | bytes 9220 | tf_op jit(solution)/shard_map/all_to_all | solution.py:118
  68.4 0.8 copy.132
  69.3 1.4 %mul.94 = f32[8,48,3,128]{3,2,1,0:T(4,128)S(1)} broadcast(f32[8,48,3]{2,1,0:T(8,128)} %copy.132), dimensions={0,1,2} | broadcast | bytes 594432 | tf_op jit(solution)/shard_map/mul | solution.py:71
  70.7 1.2 mul.95
  71.8 1.3 %fusion.6 = f32[3,6,8,128]{3,2,1,0:T(8,128)S(1)} fusion(bf16[512,3,128]{0,2,1:T(8,128)(2,1)} %bitcast.92, f32[3,48,512]{2,1,0:T(8,128)S(1)} %copy-done.4, f32[3,48]{1,0:T(4,128)S(1)} %get-tuple-element.55, f32[48,3]{0,1:T(4,128)S(1)} %get-tuple-element.39, f32[48,3]{0,1:T(4,128)S(1)} %bitcast.98), kind=kOutput, calls=%fused_computation.12 | convolution fusion | flops 19058688 | bytes 763584 | tf_op jit(solution)/shard_map/while/body/eval_jaxpr/hqk,khd->qhd/dot_general | solution.py:35
  73.2 4.1 %all-to-all-done = f32[8,48,384]{2,1,0:T(8,128)} async-done(((f32[8,48,384]{2,1,0:T(8,128)}), f32[8,48,384]{2,1,0:T(8,128)}, u32[]{:S(2)}, u32[]{:S(2)}) %all-to-all-start) | async-done | bytes 589856 | tf_op jit(solution)/shard_map/all_to_all | solution.py:111
  77.3 1.3 %multiply_reduce_fusion = f32[48,384]{1,0:T(8,128)S(1)} fusion(f32[8,48,384]{2,1,0:T(8,128)} %all-to-all-done, f32[8,48,384]{2,1,0:T(8,128)} %mul.95), kind=kLoop, calls=%fused_computation.16 | loop fusion | flops 276480 | bytes 1253376 | tf_op jit(solution)/shard_map/reduce_sum | solution.py:70
  78.8 1.2 %convolution_convert_fusion = bf16[48,3072]{1,0:T(8,128)(2,1)} fusion(bf16[384,3072]{1,0:T(8,128)(2,1)S(1)} %copy-done, f32[48,384]{1,0:T(8,128)S(1)} %multiply_reduce_fusion, f32[6,8,3,128]{3,2,1,0:T(4,128)S(1)} %bitcast.94, f32[3,6,8,128]{3,2,1,0:T(8,128)S(1)} %fusion.6), kind=kOutput, calls=%fused_computation | convolution fusion | flops 113448960 | bytes 2875392 | tf_op jit(solution)/shard_map/dot_general | solution.py:130
  81.2 18.3 %reduce-scatter.2.cloned.1.call-done = bf16[48,768]{1,0:T(8,128)(2,1)} async-done(((bf16[48,3072]{1,0:T(8,128)(2,1)}), bf16[48,768]{1,0:T(8,128)(2,1)}) %reduce-scatter.2.cloned.1.call-update) | async-done | bytes 73744 | tf_op jit(solution)/shard_map/reduce_scatter | solution.py:131
  99.6 1.0 fusion.17
  100.6 1.2 fusion.14
  101.8 10.3 %all-reduce = (f32[48,64]{1,0:T(8,128)S(1)}, f32[64]{0:T(128)S(1)}, f32[48]{0:T(128)S(1)}, f32[48]{0:T(128)S(1)}, f32[64]{0:T(128)S(1)}) all-reduce(f32[48,64]{1,0:T(8,128)S(1)} %fusion.14, f32[64]{0:T(128)S(1)} %convolution_bitcast_fusion.2, f32[48]{0:T(128)S(1)} %get-tuple-element.27, ...), channel_id=1, replica_groups=mesh['seq'=8,'head'=4] {'head'}, use_global_device_ids=true, to_apply=%region_9.10 | all-reduce | flops 3296 | bytes 26368 | tf_op jit(solution)/shard_map/psum | solution.py:141
  112.1 0.9 multiply_add_fusion
  (65 shorter events, 4.3 us)
Async XLA Ops:
  7.2 71.6 %copy-start = (bf16[384,3072]{1,0:T(8,128)(2,1)S(1)}, bf16[384,3072]{1,0:T(8,128)(2,1)}, u32[]{:S(2)}) copy-start(bf16[384,3072]{1,0:T(8,128)(2,1)} %param.21) | copy-start | bytes 7077892
  8.7 1.4 %copy-start.10 = (s32[48]{0:T(128)}, s32[48]{0:T(128)S(1)}, u32[]{:S(2)}) copy-start(s32[48]{0:T(128)S(1)} %broadcast_subtract_fusion) | copy-start | bytes 580
  8.8 1.4 %copy-start.12 = (pred[128]{0:T(512)(128)(4,1)}, pred[128]{0:T(512)(128)(4,1)S(1)}, u32[]{:S(2)}) copy-start(pred[128]{0:T(512)(128)(4,1)S(1)} %fusion.31) | copy-start | bytes 388
  43.0 11.0 %copy-start.6 = (bf16[48,384]{1,0:T(8,128)(2,1)S(1)}, bf16[48,384]{1,0:T(8,128)(2,1)}, u32[]{:S(2)}) copy-start(bf16[48,384]{1,0:T(8,128)(2,1)} %param.14) | copy-start | bytes 110596
  43.7 10.7 %copy-start.7 = (f32[3,384]{1,0:T(4,128)}, f32[3,384]{1,0:T(4,128)S(1)}, u32[]{:S(2)}) copy-start(f32[3,384]{1,0:T(4,128)S(1)} %fusion.7) | copy-start | bytes 13828
  44.5 15.6 %all-to-all-start.1 = ((f32[8,1,144]{2,1,0:T(1,128)}), f32[8,1,144]{2,1,0:T(1,128)}, u32[]{:S(2)}, u32[]{:S(2)}) async-start(f32[8,1,144]{2,1,0:T(1,128)} %reshape.86), calls=%async_computation.1 | async-start | bytes 16384 | tf_op jit(solution)/shard_map/all_to_all | solution.py:118
  54.3 2.1 %copy-start.3 = (f32[3,48,512]{2,1,0:T(8,128)}, f32[3,48,512]{2,1,0:T(8,128)S(1)}, u32[]{:S(2)}) copy-start(f32[3,48,512]{2,1,0:T(8,128)S(1)} %get-tuple-element.56) | copy-start | bytes 884740
  54.3 4.8 %copy-start.2 = (bf16[1,512,384]{2,1,0:T(8,128)(2,1)S(1)}, bf16[1,512,384]{2,1,0:T(8,128)(2,1)}, u32[]{:S(2)}) copy-start(bf16[1,512,384]{2,1,0:T(8,128)(2,1)} %get-tuple-element.41) | copy-start | bytes 1179652
  60.1 11.8 %copy-start.4 = (f32[3,48,512]{2,1,0:T(8,128)S(1)}, f32[3,48,512]{2,1,0:T(8,128)}, u32[]{:S(2)}) copy-start(f32[3,48,512]{2,1,0:T(8,128)} %copy-done.3) | copy-start | bytes 884740
  60.1 17.2 %all-to-all-start = ((f32[8,48,384]{2,1,0:T(8,128)}), f32[8,48,384]{2,1,0:T(8,128)}, u32[]{:S(2)}, u32[]{:S(2)}) async-start(f32[8,48,384]{2,1,0:T(8,128)} %reshape_reshape.7), calls=%async_computation | async-start | bytes 1179648 | tf_op jit(solution)/shard_map/all_to_all | solution.py:111
  66.2 33.4 %reduce-scatter.2.cloned.1.call-start = ((), (), s32[]{:S(2)}) async-start(), calls=%async_computation.3 | async-start | bytes 368640 | tf_op jit(solution)/shard_map/reduce_scatter | solution.py:131
  73.1 7.6 %copy-start.8 = (f32[768]{0:T(1024)S(1)}, f32[768]{0:T(1024)}, u32[]{:S(2)}) copy-start(f32[768]{0:T(1024)} %param.22) | copy-start | bytes 9220
  73.1 7.6 %copy-start.9 = (f32[768]{0:T(1024)S(1)}, f32[768]{0:T(1024)}, u32[]{:S(2)}) copy-start(f32[768]{0:T(1024)} %param.23) | copy-start | bytes 9220
  73.1 7.6 %copy-start.1 = (f32[768,64]{0,1:T(8,128)S(1)}, f32[768,64]{0,1:T(8,128)}, u32[]{:S(2)}) copy-start(f32[768,64]{0,1:T(8,128)} %param.24) | copy-start | bytes 589828
  73.2 26.4 %copy-start.5 = (bf16[48,768]{1,0:T(8,128)(2,1)S(1)}, bf16[48,768]{1,0:T(8,128)(2,1)}, u32[]{:S(2)}) copy-start(bf16[48,768]{1,0:T(8,128)(2,1)} %param.20) | copy-start | bytes 221188
  78.6 33.5 %copy-start.11 = (s32[48]{0:T(128)S(1)}, s32[48]{0:T(128)}, u32[]{:S(2)}) copy-start(s32[48]{0:T(128)} %copy-done.10) | copy-start | bytes 580
  78.6 33.5 %copy-start.13 = (pred[128]{0:T(512)(128)(4,1)S(1)}, pred[128]{0:T(512)(128)(4,1)}, u32[]{:S(2)}) copy-start(pred[128]{0:T(512)(128)(4,1)} %copy-done.12) | copy-start | bytes 388
  78.6 33.5 %copy-start.14 = (f32[128,64]{0,1:T(8,128)S(1)}, f32[128,64]{0,1:T(8,128)}, u32[]{:S(2)}) copy-start(f32[128,64]{0,1:T(8,128)} %param.25) | copy-start | bytes 98308
  78.6 33.5 %copy-start.15 = (f32[128,64]{0,1:T(8,128)S(1)}, f32[128,64]{0,1:T(8,128)}, u32[]{:S(2)}) copy-start(f32[128,64]{0,1:T(8,128)} %param.26) | copy-start | bytes 98308
Sparse Core Ops, SparseCore 0:
  80.2 19.3 reduce-scatter.1
where the time goes:
time: 121 us; the launch traced here: 120 us
  blocking collectives  43.1 us (36%)
  waiting for transfers between devices  22.5 us (19%)
  between operations  15.8 us (13%)
  local copies, waits for them, and re-layouts  12.8 us (11%)
  starting transfers between devices  11.8 us (10%)
  matrix products  9.06 us (7%)
  other arithmetic  4.9 us (4%)
    all_gather x1, blocking collectives, on_device(): gathered = lax.all_gather(query, 'seq', axis=0, tiled=True)  32.8 us
    reduce_scatter x1, waiting for transfers between devices, on_device(): lax.psum_scatter(col_terms.astype(jnp.bfloat16), 'head', scatter_dimensio...  18.3 us
    psum x1, blocking collectives, on_device(): lax.psum((scaled_part, column_part, offset_part, row_sums, row_squares),...  10.3 us
    all_to_all x1, starting transfers between devices, on_device(): lax.all_to_all(blended.reshape(shards, slot_count, row_width), 'seq', spl...  6.13 us
    all_to_all x1, starting transfers between devices, on_device(): lax.all_to_all(spread.reshape(shards, slot_count, head_count), 'seq', spl...  5.6 us
    all_to_all x1, waiting for transfers between devices, on_device(): lax.all_to_all(blended.reshape(shards, slot_count, row_width), 'seq', spl...  4.11 us
    dot_general x2, matrix products, one_block(): jnp.einsum('hqk,khd->qhd', weights.astype(jnp.bfloat16), values_split, pr...  3.36 us
    unnamed x37, local copies, waits for them, and re-layouts  2.95 us
  transfers between devices with their start and end apart: 3, of which 2 were waited for; matrix products, arithmetic and copies ran while one was open for 14% of the time, Pallas kernels for 0%

commit v1 on v0

v1 whole, which is shorter than its diff:
```python
import functools

import jax
import jax.numpy as jnp
from jax import lax
from jax.experimental import pallas as pl
from jax.experimental.pallas import tpu as pltpu
from jax.sharding import PartitionSpec as P

HD = 128
EPS = 1e-06
MESH = pl.DeviceIdType.MESH
HIGH = lax.Precision.HIGHEST


def loop(first, last, body, carry):
    if last - first <= 8:
        for d in range(first, last):
            carry = body(d, carry)
        return carry
    return lax.fori_loop(first, last, body, carry)


def kernel(
    n_seq,
    n_head,
    pair,
    query,
    new_kv,
    cache_kv,
    text_hbm,
    active,
    counts,
    hidden,
    w_out_hbm,
    mod_shift,
    mod_scale,
    w_final,
    latent,
    cached_velocity,
    step_size,
    velocity,
    latent_next,
    q_all,
    kv,
    text,
    w_out,
    part_send,
    part_recv,
    stat_send,
    stat_recv,
    cols_send,
    cols_recv,
    sums,
    local_sem,
    kv_send_sem,
    kv_recv_sem,
    q_send_sem,
    q_recv_sem,
    part_send_sem,
    part_recv_sem,
    stat_send_sem,
    stat_recv_sem,
    cols_send_sem,
    cols_recv_sem,
    sums_send_sem,
    sums_recv_sem,
):
    seq = lax.axis_index("seq")
    head = lax.axis_index("head")
    slots, width = query.shape
    tokens = cache_kv.shape[1]
    heads = width // HD
    groups = n_seq // pair
    group = seq // pair
    place = seq % pair
    model = n_head * hidden.shape[1]
    share = hidden.shape[1]
    channels = w_final.shape[1]

    def group_peer(d):
        return lax.rem(group + d, groups)

    def head_peer(d):
        return lax.rem(head + d, n_head)

    barrier = pltpu.get_barrier_semaphore()

    def greet(d, carry):
        pl.semaphore_signal(
            barrier, inc=1, device_id=(group_peer(d) * pair + place, head), device_id_type=MESH
        )
        return carry

    loop(1, groups, greet, 0)
    partner = group * pair + (pair - 1 - place)
    if pair == 2:
        pl.semaphore_signal(barrier, inc=1, device_id=(partner, head), device_id_type=MESH)
    for d in range(1, n_head):
        pl.semaphore_signal(barrier, inc=1, device_id=(seq, head_peer(d)), device_id_type=MESH)

    local = [pltpu.make_async_copy(text_hbm, text, local_sem.at[0])]
    for d in range(n_head):
        at = pl.ds(pl.multiple_of(head_peer(d) * share, 128), share)
        local.append(
            pltpu.make_async_copy(w_out_hbm.at[:, at], w_out.at[d], local_sem.at[1 + d])
        )
    for copy in local:
        copy.start()

    positions = active[...] - seq * tokens
    slot_ids = lax.broadcasted_iota(jnp.int32, (1, slots), 1)
    positions = jnp.where(slot_ids < counts[0], positions, -1)
    matched = lax.broadcasted_iota(jnp.int32, (tokens, slots), 0) == positions
    one_hot = matched.astype(jnp.float32)
    replaced = jnp.max(one_hot, axis=1, keepdims=True) > 0.5

    def place_rows(which):
        placed = jnp.dot(
            one_hot.astype(jnp.bfloat16), new_kv[which], preferred_element_type=jnp.float32
        )
        own = cache_kv[which].astype(jnp.float32)
        kv[which, 0] = jnp.where(replaced, placed, own).astype(jnp.bfloat16)

    place_rows(0)
    place_rows(1)

    pl.semaphore_wait(barrier, groups - 1 + pair - 1 + n_head - 1)

    def q_copy(d):
        return pltpu.make_async_remote_copy(
            src_ref=query,
            dst_ref=q_all.at[group],
            send_sem=q_send_sem.at[d],
            recv_sem=q_recv_sem.at[group],
            device_id=(group_peer(d) * pair + place, head),
            device_id_type=MESH,
        )

    def kv_copy(which):
        return pltpu.make_async_remote_copy(
            src_ref=kv.at[which, 0],
            dst_ref=kv.at[which, 1],
            send_sem=kv_send_sem.at[which],
            recv_sem=kv_recv_sem.at[which],
            device_id=(partner, head),
            device_id_type=MESH,
        )

    def start_q(d, carry):
        q_copy(d).start()
        return carry

    if pair == 2:
        kv_copy(0).start()
    loop(1, groups, start_q, 0)
    if pair == 2:
        kv_copy(1).start()

    def attend(rows, keys, values):
        result = []
        for h in range(heads):
            at = slice(h * HD, (h + 1) * HD)
            scores = lax.dot_general(
                rows[:, at],
                keys[:, at],
                (((1,), (1,)), ((), ())),
                preferred_element_type=jnp.float32,
            ) * HD ** (-0.5)
            top = jnp.max(scores, axis=1, keepdims=True)
            weights = jnp.exp(scores - top)
            total = jnp.sum(weights, axis=1, keepdims=True)
            blend = jnp.dot(
                weights.astype(jnp.bfloat16), values[:, at], preferred_element_type=jnp.float32
            )
            result.append((blend, top, total))
        return result

    def merge(first, second):
        result = []
        for (blend_a, top_a, total_a), (blend_b, top_b, total_b) in zip(first, second):
            top = jnp.maximum(top_a, top_b)
            share_a, share_b = jnp.exp(top_a - top), jnp.exp(top_b - top)
            result.append(
                (
                    blend_a * share_a + blend_b * share_b,
                    top,
                    total_a * share_a + total_b * share_b,
                )
            )
        return result

    lifted = 1.0 + mod_scale[...]
    rows8 = lax.broadcasted_iota(jnp.int32, (8, share), 0)
    pairs = jnp.where(rows8 == 0, lifted, jnp.where(rows8 == 1, mod_shift[...], 0.0))
    sums[head, slots : slots + 8, 0:channels] = jnp.dot(
        pairs, w_final[...], precision=HIGH, preferred_element_type=jnp.float32
    )
    local[0].wait()
    state = attend(query[...], text[0], text[1])

    if pair == 2:
        kv_copy(0).wait_recv()
        kv_copy(1).wait_recv()
    keys = kv[0].reshape(pair * tokens, width)
    values = kv[1].reshape(pair * tokens, width)

    def part_copy(d):
        return pltpu.make_async_remote_copy(
            src_ref=part_send.at[d],
            dst_ref=part_recv.at[group],
            send_sem=part_send_sem.at[d],
            recv_sem=part_recv_sem.at[group],
            device_id=(group_peer(d) * pair + place, head),
            device_id_type=MESH,
        )

    def stat_copy(d):
        return pltpu.make_async_remote_copy(
            src_ref=stat_send.at[d],
            dst_ref=stat_recv.at[group],
            send_sem=stat_send_sem.at[d],
            recv_sem=stat_recv_sem.at[group],
            device_id=(group_peer(d) * pair + place, head),
            device_id_type=MESH,
        )

    def arrived(buffer, sems, source):
        pltpu.make_async_remote_copy(
            src_ref=buffer.at[source],
            dst_ref=buffer.at[source],
            send_sem=q_send_sem.at[0],
            recv_sem=sems.at[source],
            device_id=(source * pair + place, head),
            device_id_type=MESH,
        ).wait_recv()

    lanes = lax.broadcasted_iota(jnp.int32, (slots, HD), 1)

    def answer(d, carry):
        source = group_peer(d)
        arrived(q_all, q_recv_sem, source)
        spread = jnp.zeros((slots, HD), jnp.float32)
        for h, (blend, top, total) in enumerate(attend(q_all[source], keys, values)):
            part_send[d, :, h * HD : (h + 1) * HD] = (blend / total).astype(jnp.bfloat16)
            spread = jnp.where(lanes == h, top + jnp.log(total), spread)
        stat_send[d] = jnp.transpose(spread)[:8]
        stat_copy(d).start()
        part_copy(d).start()
        return carry

    loop(1, groups, answer, 0)
    state = merge(state, attend(query[...], keys, values))

    def gather(d, carry):
        source = lax.rem(group + groups - d, groups)
        arrived(stat_recv, stat_recv_sem, source)
        arrived(part_recv, part_recv_sem, source)
        spread = jnp.transpose(stat_recv[source])
        other = [
            (
                part_recv[source, :, h * HD : (h + 1) * HD].astype(jnp.float32),
                spread[:, h : h + 1],
                jnp.ones((slots, 1), jnp.float32),
            )
            for h in range(heads)
        ]
        return merge(carry, other)

    state = loop(1, groups, gather, state)
    attended = jnp.concatenate(
        [(blend / total).astype(jnp.bfloat16) for blend, top, total in state], axis=1
    )

    def cols_copy(d):
        return pltpu.make_async_remote_copy(
            src_ref=cols_send.at[d],
            dst_ref=cols_recv.at[d],
            send_sem=cols_send_sem.at[d],
            recv_sem=cols_recv_sem.at[d],
            device_id=(seq, head_peer(d)),
            device_id_type=MESH,
        )

    for d in range(1, n_head):
        local[1 + d].wait()
        cols_send[d] = jnp.dot(attended, w_out[d], preferred_element_type=jnp.float32).astype(
            jnp.bfloat16
        )
        cols_copy(d).start()
    local[1].wait()
    residual = hidden[...].astype(jnp.float32) + jnp.dot(
        attended, w_out[0], preferred_element_type=jnp.float32
    )
    for d in range(1, n_head):
        cols_copy(d).wait_recv()
        residual = residual + cols_recv[d].astype(jnp.float32)

    mean_here = jnp.sum(residual, axis=1, keepdims=True) / share
    centred = residual - mean_here
    square_here = jnp.sum(centred * centred, axis=1, keepdims=True)
    scaled = jnp.dot(
        centred * lifted, w_final[...], precision=HIGH, preferred_element_type=jnp.float32
    )
    sums[head, 0:slots, 0:channels] = scaled
    sums[head, 0:slots, channels : channels + 1] = mean_here
    sums[head, 0:slots, channels + 1 : channels + 2] = square_here

    def sums_copy(d):
        return pltpu.make_async_remote_copy(
            src_ref=sums.at[head],
            dst_ref=sums.at[head],
            send_sem=sums_send_sem.at[d],
            recv_sem=sums_recv_sem.at[head],
            device_id=(seq, head_peer(d)),
            device_id_type=MESH,
        )

    for d in range(1, n_head):
        sums_copy(d).start()
    for d in range(1, n_head):
        source = head_peer(d)
        pltpu.make_async_remote_copy(
            src_ref=sums.at[source],
            dst_ref=sums.at[source],
            send_sem=sums_send_sem.at[0],
            recv_sem=sums_recv_sem.at[source],
            device_id=(seq, source),
            device_id_type=MESH,
        ).wait_recv()

    means = [sums[i, 0:slots, channels : channels + 1] for i in range(n_head)]
    mean = sum(means[1:], means[0]) / n_head
    squares = jnp.zeros((slots, 1), jnp.float32)
    fresh = jnp.zeros((slots, channels), jnp.float32)
    offset = jnp.zeros((1, channels), jnp.float32)
    for i in range(n_head):
        away = means[i] - mean
        squares = squares + sums[i, 0:slots, channels + 1 : channels + 2] + share * away * away
        column = sums[i, slots : slots + 1, 0:channels]
        fresh = fresh + sums[i, 0:slots, 0:channels] + away * column
        offset = offset + sums[i, slots + 1 : slots + 2, 0:channels]
    fresh = fresh * lax.rsqrt(squares / model + EPS) + offset
    chosen = jnp.dot(one_hot, fresh, precision=HIGH, preferred_element_type=jnp.float32)
    refreshed = jnp.where(replaced, chosen, cached_velocity[...])
    velocity[...] = refreshed
    latent_next[...] = latent[...] + step_size[0] * refreshed

    if pair == 2:
        kv_copy(0).wait_send()
        kv_copy(1).wait_send()

    def drain(d, carry):
        q_copy(d).wait_send()
        part_copy(d).wait_send()
        stat_copy(d).wait_send()
        return carry

    loop(1, groups, drain, 0)
    for d in range(1, n_head):
        cols_copy(d).wait_send()
        sums_copy(d).wait_send()


def on_device(
    n_seq,
    n_head,
    query,
    new_kv,
    cache_kv,
    text_kv,
    active,
    counts,
    hidden,
    w_out,
    mod_shift,
    mod_scale,
    w_final,
    latent,
    cached_velocity,
    step_size,
):
    slots, width = query.shape
    tokens = cache_kv.shape[1]
    share = hidden.shape[1]
    channels = w_final.shape[1]
    pair = 2 if n_seq % 2 == 0 else 1
    groups = n_seq // pair
    vmem = pl.BlockSpec(memory_space=pltpu.VMEM)
    smem = pl.BlockSpec(memory_space=pltpu.SMEM)
    hbm = pl.BlockSpec(memory_space=pl.ANY)
    dma = pltpu.SemaphoreType.DMA
    flops = 2 * slots * (2 * width * (n_seq * tokens + text_kv.shape[1]) + width * share * n_head)
    return pl.pallas_call(
        functools.partial(kernel, n_seq, n_head, pair),
        out_shape=(
            jax.ShapeDtypeStruct(latent.shape, jnp.float32),
            jax.ShapeDtypeStruct(latent.shape, jnp.float32),
        ),
        in_specs=[
            vmem,
            vmem,
            vmem,
            hbm,
            vmem,
            smem,
            vmem,
            hbm,
            vmem,
            vmem,
            vmem,
            vmem,
            vmem,
            smem,
        ],
        out_specs=(vmem, vmem),
        scratch_shapes=[
            pltpu.VMEM((groups, slots, width), jnp.bfloat16),
            pltpu.VMEM((2, pair, tokens, width), jnp.bfloat16),
            pltpu.VMEM(text_kv.shape, jnp.bfloat16),
            pltpu.VMEM((n_head, width, share), jnp.bfloat16),
            pltpu.VMEM((groups, slots, width), jnp.bfloat16),
            pltpu.VMEM((groups, slots, width), jnp.bfloat16),
            pltpu.VMEM((groups, 8, slots), jnp.float32),
            pltpu.VMEM((groups, 8, slots), jnp.float32),
            pltpu.VMEM((n_head, slots, share), jnp.bfloat16),
            pltpu.VMEM((n_head, slots, share), jnp.bfloat16),
            pltpu.VMEM((n_head, slots + 8, 128), jnp.float32),
            dma((1 + n_head,)),
            dma((2,)),
            dma((2,)),
            dma((groups,)),
            dma((groups,)),
            dma((groups,)),
            dma((groups,)),
            dma((groups,)),
            dma((groups,)),
            dma((n_head,)),
            dma((n_head,)),
            dma((n_head,)),
            dma((n_head,)),
        ],
        compiler_params=pltpu.CompilerParams(
            collective_id=0, has_side_effects=True, vmem_limit_bytes=40 * 1024 * 1024
        ),
        cost_estimate=pl.CostEstimate(
            flops=flops, bytes_accessed=2 * w_out.size, transcendentals=0
        ),
    )(
        query,
        new_kv,
        cache_kv,
        text_kv,
        active.reshape(1, slots),
        counts,
        hidden,
        w_out,
        mod_shift.reshape(1, share),
        mod_scale.reshape(1, share),
        w_final,
        latent,
        cached_velocity,
        step_size,
    )


def solution(mesh):
    in_specs = (
        P("seq", "head"),
        P(None, "seq", "head"),
        P(None, "seq", "head"),
        P(None, None, "head"),
        P("seq"),
        P("seq"),
        P("seq", "head"),
        P("head", None),
        P("head"),
        P("head"),
        P("head", None),
        P("seq", None),
        P("seq", None),
        P(),
    )
    out_specs = (P("seq", None), P("seq", None))
    return jax.shard_map(
        functools.partial(on_device, mesh.shape["seq"], mesh.shape["head"]),
        mesh=mesh,
        in_specs=in_specs,
        out_specs=out_specs,
        check_vma=False,
    )
```

time: 121 us -> 41.2 us (0.34)
  blocking collectives: 43.1 us -> 0 us
  Pallas kernels: 0 us -> 26.2 us
  waiting for transfers between devices: 22.5 us -> 0 us
  between operations: 15.8 us -> 1.96 us
  starting transfers between devices: 11.8 us -> 0 us
  matrix products: 9.06 us -> 0 us
  other arithmetic: 4.9 us -> 0 us
    all_gather x1 -> x0, blocking collectives: 32.8 us -> none  [on_device(): gathered = lax.all_gather(query, 'seq', axis=0, tiled=True)]
    pallas_call x0 -> x1, Pallas kernels: none -> 26.2 us  [on_device(): pl.pallas_call(functools.partial(kernel, n_seq, n_head, pair), out_shape=...]
    reduce_scatter x1 -> x0, waiting for transfers between devices: 18.3 us -> none  [on_device(): lax.psum_scatter(col_terms.astype(jnp.bfloat16), 'head', scatter_dimensio...]
    all_to_all x2 -> x0, starting transfers between devices: 11.7 us -> none  [the longest x1 6.13 us: on_device(): lax.all_to_all(blended.reshape(shards, slot_count, row_width), 'seq', spl...]
    psum x1 -> x0, blocking collectives: 10.3 us -> none  [on_device(): lax.psum((scaled_part, column_part, offset_part, row_sums, row_squares),...]
    dot_general x10 -> x0, matrix products: 9.06 us -> none  [the longest x2 3.36 us: one_block(): jnp.einsum('hqk,khd->qhd', weights.astype(jnp.bfloat16), values_split, pr...]
    unnamed x37 -> x17, local copies, waits for them, and re-layouts: 2.95 us -> 9.71 us
    all_to_all x2 -> x0, waiting for transfers between devices: 4.11 us -> none  [the longest x1 4.11 us: on_device(): lax.all_to_all(blended.reshape(shards, slot_count, row_width), 'seq', spl...]
  transfers between devices with their start and end apart: 3 -> 0, of which waited for: 2 -> 0; matrix products, arithmetic and copies ran while one was open for 14% -> 0% of each run, Pallas kernels for 0% -> 0%
where the time goes in v1:
time: 41.2 us; the launch traced here: 40.6 us
  Pallas kernels  26.2 us (64%)
  local copies, waits for them, and re-layouts  12.5 us (30%)
  between operations  1.96 us (5%)
    pallas_call x1, Pallas kernels, on_device(): pl.pallas_call(functools.partial(kernel, n_seq, n_head, pair), out_shape=...  26.2 us
    unnamed x17, local copies, waits for them, and re-layouts  9.71 us
    pallas_call x2, local copies, waits for them, and re-layouts, on_device(): pl.pallas_call(functools.partial(kernel, n_seq, n_head, pair), out_shape=...  1.4 us

profile of v1, /device:TPU:0, one launch (start us, length us, event | category | flops | bytes accessed | tf_op | source)
XLA Modules:
  0.0 40.6 jit_solution(1384577066215200694)
XLA Ops:
  1.9 0.7 %reshape.14.mod_shift = f32[1,768]{1,0:T(1,128)S(1)} reshape(f32[768]{0:T(1024)} %param.22) | data formatting | bytes 6144 | tf_op jit(solution)/shard_map/reshape | solution.py:458
  2.6 0.7 %reshape.15.mod_scale = f32[1,768]{1,0:T(1,128)S(1)} reshape(f32[768]{0:T(1024)} %param.23) | data formatting | bytes 6144 | tf_op jit(solution)/shard_map/reshape | solution.py:459
  3.3 0.8 %copy.17.latent = f32[128,64]{1,0:T(8,128)S(1)} copy(f32[128,64]{0,1:T(8,128)} %param.25) | data formatting | bytes 65536 | tf_op args[11]
  4.2 0.9 %copy.18.cached_velocity = f32[128,64]{1,0:T(8,128)S(1)} copy(f32[128,64]{0,1:T(8,128)} %param.26) | data formatting | bytes 65536 | tf_op args[12]
  5.0 1.1 %copy.16.w_final = f32[768,64]{1,0:T(8,128)S(1)} copy(f32[768,64]{0,1:T(8,128)} %param.24) | data formatting | bytes 393216 | tf_op args[10]
  6.1 0.0 copy-start
  6.1 1.7 %copy-done = bf16[384,3072]{1,0:T(8,128)(2,1)S(1)} copy-done((bf16[384,3072]{1,0:T(8,128)(2,1)S(1)}, bf16[384,3072]{1,0:T(8,128)(2,1)}, u32[]{:S(2)}) %copy-start) | copy-done | bytes 2359320
  7.8 0.0 copy-start.1
  7.8 1.1 %copy-done.1 = bf16[2,512,384]{2,1,0:T(8,128)(2,1)S(1)} copy-done((bf16[2,512,384]{2,1,0:T(8,128)(2,1)S(1)}, bf16[2,512,384]{2,1,0:T(8,128)(2,1)}, u32[]{:S(2)}) %copy-start.1) | copy-done | bytes 786456
  8.9 0.0 copy-start.2
  8.9 0.9 %copy-done.2 = bf16[2,128,384]{2,1,0:T(8,128)(2,1)S(1)} copy-done((bf16[2,128,384]{2,1,0:T(8,128)(2,1)S(1)}, bf16[2,128,384]{2,1,0:T(8,128)(2,1)}, u32[]{:S(2)}) %copy-start.2) | copy-done | bytes 196632
  9.8 0.0 copy-start.3
  9.8 0.9 %copy-done.3 = bf16[2,48,384]{2,1,0:T(8,128)(2,1)S(1)} copy-done((bf16[2,48,384]{2,1,0:T(8,128)(2,1)S(1)}, bf16[2,48,384]{2,1,0:T(8,128)(2,1)}, u32[]{:S(2)}) %copy-start.3) | copy-done | bytes 73752
  10.7 0.0 copy-start.4
  10.7 0.9 %copy-done.4 = bf16[48,768]{1,0:T(8,128)(2,1)S(1)} copy-done((bf16[48,768]{1,0:T(8,128)(2,1)S(1)}, bf16[48,768]{1,0:T(8,128)(2,1)}, u32[]{:S(2)}) %copy-start.4) | copy-done | bytes 73752
  11.6 0.0 copy-start.5
  11.6 0.8 %copy-done.5 = bf16[48,384]{1,0:T(8,128)(2,1)S(1)} copy-done((bf16[48,384]{1,0:T(8,128)(2,1)S(1)}, bf16[48,384]{1,0:T(8,128)(2,1)}, u32[]{:S(2)}) %copy-start.5) | copy-done | bytes 36888
  12.4 0.0 copy-start.6
  12.4 0.7 %copy-done.6 = s32[48]{0:T(128)S(1)} copy-done((s32[48]{0:T(128)S(1)}, s32[48]{0:T(128)}, u32[]{:S(2)}) %copy-start.6) | copy-done | bytes 216
  13.0 26.2 %shard_map.149 = (f32[128,64]{1,0:T(8,128)S(1)}, f32[128,64]{1,0:T(8,128)S(1)}) custom-call(bf16[48,384]{1,0:T(8,128)(2,1)S(1)} %copy-done.5, bf16[2,48,384]{2,1,0:T(8,128)(2,1)S(1)} %copy-done.3, bf16[2,128,384]{2,1,0:T(8,128)(2,1)S(1)} %copy-done.2, bf16[2,512,384]{2,1,0:T(8,128)(2,1)S(1)} %copy-done.1, s32[1,48]{1,0:T(1,128)S(1)} %bitcast.1, ...), custom_call_target="tpu_custom_call" | custom-call | flops 226492416 | bytes 2359296 | tf_op jit(solution)/shard_map/pallas_call | solution.py:394
  39.2 0.7 %copy.19 = f32[128,64]{0,1:T(8,128)} copy(f32[128,64]{1,0:T(8,128)S(1)} %get-tuple-element.2) | data formatting | bytes 65536 | tf_op jit(solution)/shard_map/pallas_call | solution.py:394
  39.9 0.7 %copy.20 = f32[128,64]{0,1:T(8,128)} copy(f32[128,64]{1,0:T(8,128)S(1)} %get-tuple-element.3) | data formatting | bytes 65536 | tf_op jit(solution)/shard_map/pallas_call | solution.py:394
Async XLA Ops:
  6.1 1.7 %copy-start = (bf16[384,3072]{1,0:T(8,128)(2,1)S(1)}, bf16[384,3072]{1,0:T(8,128)(2,1)}, u32[]{:S(2)}) copy-start(bf16[384,3072]{1,0:T(8,128)(2,1)} %w_out_hbm.1) | copy-start | bytes 7077892
  7.8 1.1 %copy-start.1 = (bf16[2,512,384]{2,1,0:T(8,128)(2,1)S(1)}, bf16[2,512,384]{2,1,0:T(8,128)(2,1)}, u32[]{:S(2)}) copy-start(bf16[2,512,384]{2,1,0:T(8,128)(2,1)} %text_hbm.1) | copy-start | bytes 2359300
  8.9 0.9 %copy-start.2 = (bf16[2,128,384]{2,1,0:T(8,128)(2,1)S(1)}, bf16[2,128,384]{2,1,0:T(8,128)(2,1)}, u32[]{:S(2)}) copy-start(bf16[2,128,384]{2,1,0:T(8,128)(2,1)} %cache_kv.1) | copy-start | bytes 589828
  9.8 0.9 %copy-start.3 = (bf16[2,48,384]{2,1,0:T(8,128)(2,1)S(1)}, bf16[2,48,384]{2,1,0:T(8,128)(2,1)}, u32[]{:S(2)}) copy-start(bf16[2,48,384]{2,1,0:T(8,128)(2,1)} %new_kv.1) | copy-start | bytes 221188
  10.7 0.9 %copy-start.4 = (bf16[48,768]{1,0:T(8,128)(2,1)S(1)}, bf16[48,768]{1,0:T(8,128)(2,1)}, u32[]{:S(2)}) copy-start(bf16[48,768]{1,0:T(8,128)(2,1)} %hidden.1) | copy-start | bytes 221188
  11.6 0.8 %copy-start.5 = (bf16[48,384]{1,0:T(8,128)(2,1)S(1)}, bf16[48,384]{1,0:T(8,128)(2,1)}, u32[]{:S(2)}) copy-start(bf16[48,384]{1,0:T(8,128)(2,1)} %query.1) | copy-start | bytes 110596
  12.4 0.7 %copy-start.6 = (s32[48]{0:T(128)S(1)}, s32[48]{0:T(128)}, u32[]{:S(2)}) copy-start(s32[48]{0:T(128)} %param.18) | copy-start | bytes 580

commit v2 on v1

--- a/solution.py
+++ b/solution.py
@@ -25,22 +25,28 @@
     n_seq,
     n_head,
     pair,
+    query_hbm,
+    new_kv_hbm,
+    cache_kv_hbm,
+    text_hbm,
+    active_hbm,
+    counts_hbm,
+    hidden_hbm,
+    w_out_hbm,
+    mod_shift_hbm,
+    mod_scale_hbm,
+    w_final_hbm,
+    chosen,
+    renewed,
     query,
     new_kv,
     cache_kv,
-    text_hbm,
     active,
     counts,
     hidden,
-    w_out_hbm,
     mod_shift,
     mod_scale,
     w_final,
-    latent,
-    cached_velocity,
-    step_size,
-    velocity,
-    latent_next,
     q_all,
     kv,
     text,
@@ -76,7 +82,7 @@
     place = seq % pair
     model = n_head * hidden.shape[1]
     share = hidden.shape[1]
-    channels = w_final.shape[1]
+    channels = w_final.shape[0]
 
     def group_peer(d):
         return lax.rem(group + d, groups)
@@ -99,14 +105,34 @@
     for d in range(1, n_head):
         pl.semaphore_signal(barrier, inc=1, device_id=(seq, head_peer(d)), device_id_type=MESH)
 
-    local = [pltpu.make_async_copy(text_hbm, text, local_sem.at[0])]
-    for d in range(n_head):
+    local = []
+
+    def fetch(source, target):
+        copy = pltpu.make_async_copy(source, target, local_sem.at[len(local)])
+        copy.start()
+        local.append(copy)
+        return copy
+
+    first_in = [
+        fetch(query_hbm, query),
+        fetch(active_hbm, active),
+        fetch(counts_hbm, counts),
+        fetch(new_kv_hbm, new_kv),
+        fetch(cache_kv_hbm, cache_kv),
+    ]
+    text_in = fetch(text_hbm, text)
+    norm_in = [
+        fetch(mod_shift_hbm, mod_shift),
+        fetch(mod_scale_hbm, mod_scale),
+        fetch(w_final_hbm, w_final),
+    ]
+    w_out_in = [None] * n_head
+    for d in [*range(1, n_head), 0]:
         at = pl.ds(pl.multiple_of(head_peer(d) * share, 128), share)
-        local.append(
-            pltpu.make_async_copy(w_out_hbm.at[:, at], w_out.at[d], local_sem.at[1 + d])
-        )
-    for copy in local:
-        copy.start()
+        w_out_in[d] = fetch(w_out_hbm.at[:, at], w_out.at[d])
+    hidden_in = fetch(hidden_hbm, hidden)
+    for copy in first_in:
+        copy.wait()
 
     positions = active[...] - seq * tokens
     slot_ids = lax.broadcasted_iota(jnp.int32, (1, slots), 1)
@@ -124,6 +150,9 @@
 
     place_rows(0)
     place_rows(1)
+    renewed[...] = jnp.transpose(
+        jnp.broadcast_to(replaced.astype(jnp.float32), (tokens, channels))
+    )
 
     pl.semaphore_wait(barrier, groups - 1 + pair - 1 + n_head - 1)
 
@@ -190,13 +219,27 @@
             )
         return result
 
-    lifted = 1.0 + mod_scale[...]
+    for copy in norm_in:
+        copy.wait()
+
+    def as_row(ref):
+        return jnp.concatenate([ref[i : i + 1, :] for i in range(ref.shape[0])], axis=1)
+
+    lifted = 1.0 + as_row(mod_scale)
+
+    def final_dot(rows):
+        return lax.dot_general(
+            rows,
+            w_final[...],
+            (((1,), (1,)), ((), ())),
+            precision=HIGH,
+            preferred_element_type=jnp.float32,
+        )
+
     rows8 = lax.broadcasted_iota(jnp.int32, (8, share), 0)
-    pairs = jnp.where(rows8 == 0, lifted, jnp.where(rows8 == 1, mod_shift[...], 0.0))
-    sums[head, slots : slots + 8, 0:channels] = jnp.dot(
-        pairs, w_final[...], precision=HIGH, preferred_element_type=jnp.float32
-    )
-    local[0].wait()
+    pairs = jnp.where(rows8 == 0, lifted, jnp.where(rows8 == 1, as_row(mod_shift), 0.0))
+    sums[head, slots : slots + 8, 0:channels] = final_dot(pairs)
+    text_in.wait()
     state = attend(query[...], text[0], text[1])
 
     if pair == 2:
@@ -283,12 +326,13 @@
         )
 
     for d in range(1, n_head):
-        local[1 + d].wait()
+        w_out_in[d].wait()
         cols_send[d] = jnp.dot(attended, w_out[d], preferred_element_type=jnp.float32).astype(
             jnp.bfloat16
         )
         cols_copy(d).start()
-    local[1].wait()
+    w_out_in[0].wait()
+    hidden_in.wait()
     residual = hidden[...].astype(jnp.float32) + jnp.dot(
         attended, w_out[0], preferred_element_type=jnp.float32
     )
@@ -299,9 +343,7 @@
     mean_here = jnp.sum(residual, axis=1, keepdims=True) / share
     centred = residual - mean_here
     square_here = jnp.sum(centred * centred, axis=1, keepdims=True)
-    scaled = jnp.dot(
-        centred * lifted, w_final[...], precision=HIGH, preferred_element_type=jnp.float32
-    )
+    scaled = final_dot(centred * lifted)
     sums[head, 0:slots, 0:channels] = scaled
     sums[head, 0:slots, channels : channels + 1] = mean_here
     sums[head, 0:slots, channels + 1 : channels + 2] = square_here
@@ -341,10 +383,9 @@
         fresh = fresh + sums[i, 0:slots, 0:channels] + away * column
         offset = offset + sums[i, slots + 1 : slots + 2, 0:channels]
     fresh = fresh * lax.rsqrt(squares / model + EPS) + offset
-    chosen = jnp.dot(one_hot, fresh, precision=HIGH, preferred_element_type=jnp.float32)
-    refreshed = jnp.where(replaced, chosen, cached_velocity[...])
-    velocity[...] = refreshed
-    latent_next[...] = latent[...] + step_size[0] * refreshed
+    chosen[...] = jnp.transpose(
+        jnp.dot(one_hot, fresh, precision=HIGH, preferred_element_type=jnp.float32)
+    )
 
     if pair == 2:
         kv_copy(0).wait_send()
@@ -387,34 +428,27 @@
     pair = 2 if n_seq % 2 == 0 else 1
     groups = n_seq // pair
     vmem = pl.BlockSpec(memory_space=pltpu.VMEM)
-    smem = pl.BlockSpec(memory_space=pltpu.SMEM)
-    hbm = pl.BlockSpec(memory_space=pl.ANY)
+    hbm = pl.BlockSpec(memory_space=pltpu.HBM)
     dma = pltpu.SemaphoreType.DMA
     flops = 2 * slots * (2 * width * (n_seq * tokens + text_kv.shape[1]) + width * share * n_head)
-    return pl.pallas_call(
+    chosen, renewed = pl.pallas_call(
         functools.partial(kernel, n_seq, n_head, pair),
         out_shape=(
-            jax.ShapeDtypeStruct(latent.shape, jnp.float32),
-            jax.ShapeDtypeStruct(latent.shape, jnp.float32),
+            jax.ShapeDtypeStruct((channels, tokens), jnp.float32),
+            jax.ShapeDtypeStruct((channels, tokens), jnp.float32),
         ),
-        in_specs=[
-            vmem,
-            vmem,
-            vmem,
-            hbm,
-            vmem,
-            smem,
-            vmem,
-            hbm,
-            vmem,
-            vmem,
-            vmem,
-            vmem,
-            vmem,
-            smem,
-        ],
+        in_specs=[hbm] * 11,
         out_specs=(vmem, vmem),
         scratch_shapes=[
+            pltpu.VMEM(query.shape, jnp.bfloat16),
+            pltpu.VMEM(new_kv.shape, jnp.bfloat16),
+            pltpu.VMEM(cache_kv.shape, jnp.bfloat16),
+            pltpu.VMEM((1, slots), jnp.int32),
+            pltpu.SMEM((1,), jnp.int32),
+            pltpu.VMEM(hidden.shape, jnp.bfloat16),
+            pltpu.VMEM((share // 128, 128), jnp.float32),
+            pltpu.VMEM((share // 128, 128), jnp.float32),
+            pltpu.VMEM((channels, share), jnp.float32),
             pltpu.VMEM((groups, slots, width), jnp.bfloat16),
             pltpu.VMEM((2, pair, tokens, width), jnp.bfloat16),
             pltpu.VMEM(text_kv.shape, jnp.bfloat16),
@@ -426,7 +460,7 @@
             pltpu.VMEM((n_head, slots, share), jnp.bfloat16),
             pltpu.VMEM((n_head, slots, share), jnp.bfloat16),
             pltpu.VMEM((n_head, slots + 8, 128), jnp.float32),
-            dma((1 + n_head,)),
+            dma((10 + n_head,)),
             dma((2,)),
             dma((2,)),
             dma((groups,)),
@@ -441,7 +475,7 @@
             dma((n_head,)),
         ],
         compiler_params=pltpu.CompilerParams(
-            collective_id=0, has_side_effects=True, vmem_limit_bytes=40 * 1024 * 1024
+            collective_id=0, has_side_effects=True, vmem_limit_bytes=60 * 1024 * 1024
         ),
         cost_estimate=pl.CostEstimate(
             flops=flops, bytes_accessed=2 * w_out.size, transcendentals=0
@@ -455,13 +489,13 @@
         counts,
         hidden,
         w_out,
-        mod_shift.reshape(1, share),
-        mod_scale.reshape(1, share),
-        w_final,
-        latent,
-        cached_velocity,
-        step_size,
-    )
+        mod_shift.reshape(share // 128, 128),
+        mod_scale.reshape(share // 128, 128),
+        w_final.T,
+    )
+    velocity = jnp.where(renewed > 0.5, chosen, cached_velocity.T)
+    latent_next = latent.T + step_size[0] * velocity
+    return (velocity.T, latent_next.T)
 
 
 def solution(mesh):

time: 41.2 us -> 30.8 us (0.75)
  local copies, waits for them, and re-layouts: 12.5 us -> 0.01 us
  other arithmetic: 0 us -> 1.41 us
  Pallas kernels: 26.2 us -> 27.1 us
    unnamed x17 -> x4, local copies, waits for them, and re-layouts: 9.71 us -> 0.01 us
    transpose x0 -> x1, other arithmetic: none -> 1.41 us  [on_device(): return (velocity.T, latent_next.T)]
    pallas_call x2 -> x0, local copies, waits for them, and re-layouts: 1.4 us -> none  [on_device(): pl.pallas_call(functools.partial(kernel, n_seq, n_head, pair), out_shape=...]
    reshape x2 -> x0, local copies, waits for them, and re-layouts: 1.38 us -> none  [the longest x1 0.69 us: on_device(): mod_shift.reshape(1, share)]
    pallas_call x1, Pallas kernels: 26.2 us -> 27.1 us  [on_device(): pl.pallas_call(functools.partial(kernel, n_seq, n_head, pair), out_shape=...]
where the time goes in v2:
time: 30.8 us; the launch traced here: 30.5 us
  Pallas kernels  27.1 us (88%)
  between operations  1.97 us (6%)
  other arithmetic  1.41 us (5%)
    pallas_call x1, Pallas kernels, on_device(): pl.pallas_call(functools.partial(kernel, n_seq, n_head, pair), out_shape=...  27.1 us
    transpose x1, other arithmetic, on_device(): return (velocity.T, latent_next.T)  1.41 us

profile of v2, /device:TPU:0, one launch (start us, length us, event | category | flops | bytes accessed | tf_op | source)
XLA Modules:
  0.0 30.5 jit_solution(6596143973668670958)
XLA Ops:
  0.6 0.0 copy-start.1
  0.6 0.0 copy-start
  2.0 27.1 %shard_map.149 = (f32[64,128]{1,0:T(8,128)}, f32[64,128]{1,0:T(8,128)}) custom-call(bf16[48,384]{1,0:T(8,128)(2,1)} %query_hbm.1, bf16[2,48,384]{2,1,0:T(8,128)(2,1)} %new_kv_hbm.1, bf16[2,128,384]{2,1,0:T(8,128)(2,1)} %cache_kv_hbm.1, bf16[2,512,384]{2,1,0:T(8,128)(2,1)} %text_hbm.1, s32[1,48]{1,0:T(1,128)} %bitcast.23, s32[1]{0:T(128)S(6)} %copy.16.counts_hbm, ...), custom_call_target="tpu_custom_call" | custom-call | flops 226492416 | bytes 2359296 | tf_op jit(solution)/shard_map/pallas_call | solution.py:434
  29.1 0.0 copy-done.1
  29.1 0.0 copy-done
  29.1 1.4 %fusion = (f32[128,64]{0,1:T(8,128)}, f32[128,64]{0,1:T(8,128)}) fusion(f32[128,64]{0,1:T(8,128)S(1)} %copy-done, f32[]{:T(128)} %bitcast.19, f32[64,128]{1,0:T(8,128)} %get-tuple-element.5, f32[128,64]{0,1:T(8,128)S(1)} %copy-done.1, f32[64,128]{1,0:T(8,128)} %get-tuple-element.4), kind=kLoop, calls=%fused_computation.1 | loop fusion | flops 32768 | bytes 196612 | tf_op jit(solution)/shard_map/transpose | solution.py:498
Async XLA Ops:
  0.6 28.5 %copy-start.1 = (f32[128,64]{0,1:T(8,128)S(1)}, f32[128,64]{0,1:T(8,128)}, u32[]{:S(2)}) copy-start(f32[128,64]{0,1:T(8,128)} %param.26) | copy-start | bytes 98308
  0.6 28.5 %copy-start = (f32[128,64]{0,1:T(8,128)S(1)}, f32[128,64]{0,1:T(8,128)}, u32[]{:S(2)}) copy-start(f32[128,64]{0,1:T(8,128)} %param.25) | copy-start | bytes 98308

commit v3 on v2

--- a/solution.py
+++ b/solution.py
@@ -10,7 +10,6 @@
 HD = 128
 EPS = 1e-06
 MESH = pl.DeviceIdType.MESH
-HIGH = lax.Precision.HIGHEST
 
 
 def loop(first, last, body, carry):
@@ -36,9 +35,10 @@
     mod_shift_hbm,
     mod_scale_hbm,
     w_final_hbm,
-    chosen,
-    renewed,
-    query,
+    latent_hbm,
+    cached_velocity_hbm,
+    step_size_hbm,
+    result,
     new_kv,
     cache_kv,
     active,
@@ -47,6 +47,9 @@
     mod_shift,
     mod_scale,
     w_final,
+    latent,
+    cached_velocity,
+    step_size,
     q_all,
     kv,
     text,
@@ -74,7 +77,7 @@
 ):
     seq = lax.axis_index("seq")
     head = lax.axis_index("head")
-    slots, width = query.shape
+    slots, width = query_hbm.shape
     tokens = cache_kv.shape[1]
     heads = width // HD
     groups = n_seq // pair
@@ -87,8 +90,12 @@
     def group_peer(d):
         return lax.rem(group + d, groups)
 
+    cores = 2 if n_head % 2 == 0 else 1
+    chips = n_head // cores
+
     def head_peer(d):
-        return lax.rem(head + d, n_head)
+        chip = lax.rem(head // cores + d // cores, chips)
+        return chip * cores + lax.rem(head % cores + d % cores, cores)
 
     barrier = pltpu.get_barrier_semaphore()
 
@@ -114,7 +121,7 @@
         return copy
 
     first_in = [
-        fetch(query_hbm, query),
+        fetch(query_hbm, q_all.at[group]),
         fetch(active_hbm, active),
         fetch(counts_hbm, counts),
         fetch(new_kv_hbm, new_kv),
@@ -127,16 +134,21 @@
         fetch(w_final_hbm, w_final),
     ]
     w_out_in = [None] * n_head
-    for d in [*range(1, n_head), 0]:
+    for d in reversed(range(n_head)):
         at = pl.ds(pl.multiple_of(head_peer(d) * share, 128), share)
         w_out_in[d] = fetch(w_out_hbm.at[:, at], w_out.at[d])
     hidden_in = fetch(hidden_hbm, hidden)
+    last_in = [
+        fetch(latent_hbm, latent),
+        fetch(cached_velocity_hbm, cached_velocity),
+        fetch(step_size_hbm, step_size),
+    ]
     for copy in first_in:
         copy.wait()
 
     positions = active[...] - seq * tokens
     slot_ids = lax.broadcasted_iota(jnp.int32, (1, slots), 1)
-    positions = jnp.where(slot_ids < counts[0], positions, -1)
+    positions = jnp.where(slot_ids < counts[...], positions, -1)
     matched = lax.broadcasted_iota(jnp.int32, (tokens, slots), 0) == positions
     one_hot = matched.astype(jnp.float32)
     replaced = jnp.max(one_hot, axis=1, keepdims=True) > 0.5
@@ -150,15 +162,11 @@
 
     place_rows(0)
     place_rows(1)
-    renewed[...] = jnp.transpose(
-        jnp.broadcast_to(replaced.astype(jnp.float32), (tokens, channels))
-    )
-
     pl.semaphore_wait(barrier, groups - 1 + pair - 1 + n_head - 1)
 
     def q_copy(d):
         return pltpu.make_async_remote_copy(
-            src_ref=query,
+            src_ref=q_all.at[group],
             dst_ref=q_all.at[group],
             send_sem=q_send_sem.at[d],
             recv_sem=q_recv_sem.at[group],
@@ -186,24 +194,25 @@
     if pair == 2:
         kv_copy(1).start()
 
-    def attend(rows, keys, values):
-        result = []
-        for h in range(heads):
-            at = slice(h * HD, (h + 1) * HD)
-            scores = lax.dot_general(
-                rows[:, at],
-                keys[:, at],
-                (((1,), (1,)), ((), ())),
-                preferred_element_type=jnp.float32,
-            ) * HD ** (-0.5)
-            top = jnp.max(scores, axis=1, keepdims=True)
-            weights = jnp.exp(scores - top)
-            total = jnp.sum(weights, axis=1, keepdims=True)
-            blend = jnp.dot(
-                weights.astype(jnp.bfloat16), values[:, at], preferred_element_type=jnp.float32
-            )
-            result.append((blend, top, total))
-        return result
+    def weigh(rows, keys, h):
+        at = slice(h * HD, (h + 1) * HD)
+        scores = lax.dot_general(
+            rows[:, at],
+            keys[:, at],
+            (((1,), (1,)), ((), ())),
+            preferred_element_type=jnp.float32,
+        ) * HD ** (-0.5)
+        top = jnp.max(scores, axis=1, keepdims=True)
+        weights = jnp.exp(scores - top)
+        total = jnp.sum(weights, axis=1, keepdims=True)
+        return weights.astype(jnp.bfloat16), top, total
+
+    def blend_of(weights, values, h):
+        return jnp.dot(
+            weights,
+            values[:, h * HD : (h + 1) * HD],
+            preferred_element_type=jnp.float32,
+        )
 
     def merge(first, second):
         result = []
@@ -227,44 +236,51 @@
 
     lifted = 1.0 + as_row(mod_scale)
 
+    def split(x):
+        top = x.astype(jnp.bfloat16)
+        return top, (x - top.astype(jnp.float32)).astype(jnp.bfloat16)
+
+    final_top, final_rest = split(w_final[...])
+
     def final_dot(rows):
-        return lax.dot_general(
-            rows,
-            w_final[...],
-            (((1,), (1,)), ((), ())),
-            precision=HIGH,
-            preferred_element_type=jnp.float32,
-        )
-
-    rows8 = lax.broadcasted_iota(jnp.int32, (8, share), 0)
+        count = rows.shape[0]
+        top, rest = split(rows)
+
+        def times(left, right):
+            return lax.dot_general(
+                left, right, (((1,), (1,)), ((), ())), preferred_element_type=jnp.float32
+            )
+
+        both = times(jnp.concatenate([top, rest], axis=0), final_top)
+        return both[:count] + (both[count:] + times(top, final_rest))
+
+    rows8 = lax.broadcasted_iota(jnp.int32, (16, share), 0)
     pairs = jnp.where(rows8 == 0, lifted, jnp.where(rows8 == 1, as_row(mod_shift), 0.0))
-    sums[head, slots : slots + 8, 0:channels] = final_dot(pairs)
+    sums[head, slots : slots + 8, 0:channels] = final_dot(pairs)[:8]
     text_in.wait()
-    state = attend(query[...], text[0], text[1])
-
-    if pair == 2:
-        kv_copy(0).wait_recv()
-        kv_copy(1).wait_recv()
-    keys = kv[0].reshape(pair * tokens, width)
-    values = kv[1].reshape(pair * tokens, width)
-
-    def part_copy(d):
+    state = []
+    own = q_all[group]
+    for h in range(heads):
+        weights, top, total = weigh(own, text[0], h)
+        state.append((blend_of(weights, text[1], h), top, total))
+
+    def part_copy(to):
         return pltpu.make_async_remote_copy(
-            src_ref=part_send.at[d],
+            src_ref=part_send.at[to],
             dst_ref=part_recv.at[group],
-            send_sem=part_send_sem.at[d],
+            send_sem=part_send_sem.at[to],
             recv_sem=part_recv_sem.at[group],
-            device_id=(group_peer(d) * pair + place, head),
-            device_id_type=MESH,
-        )
-
-    def stat_copy(d):
+            device_id=(to * pair + place, head),
+            device_id_type=MESH,
+        )
+
+    def stat_copy(to):
         return pltpu.make_async_remote_copy(
-            src_ref=stat_send.at[d],
+            src_ref=stat_send.at[to],
             dst_ref=stat_recv.at[group],
-            send_sem=stat_send_sem.at[d],
+            send_sem=stat_send_sem.at[to],
             recv_sem=stat_recv_sem.at[group],
-            device_id=(group_peer(d) * pair + place, head),
+            device_id=(to * pair + place, head),
             device_id_type=MESH,
         )
 
@@ -278,37 +294,73 @@
             device_id_type=MESH,
         ).wait_recv()
 
-    lanes = lax.broadcasted_iota(jnp.int32, (slots, HD), 1)
-
-    def answer(d, carry):
-        source = group_peer(d)
-        arrived(q_all, q_recv_sem, source)
-        spread = jnp.zeros((slots, HD), jnp.float32)
-        for h, (blend, top, total) in enumerate(attend(q_all[source], keys, values)):
-            part_send[d, :, h * HD : (h + 1) * HD] = (blend / total).astype(jnp.bfloat16)
+    batch = min(groups, 4) if groups % 4 == 0 or groups < 4 else 1
+    lanes = lax.broadcasted_iota(jnp.int32, (batch * slots, HD), 1)
+
+    def answer(step, carry):
+        first = step * batch
+        for i in range(batch):
+
+            @pl.when(first + i != group)
+            def _():
+                arrived(q_all, q_recv_sem, first + i)
+
+        if pair == 2:
+
+            @pl.when(first == 0)
+            def _():
+                kv_copy(0).wait_recv()
+
+        keys = kv[0].reshape(pair * tokens, width)
+        rows = q_all[pl.ds(first, batch)].reshape(batch * slots, width)
+        weighed = [weigh(rows, keys, h) for h in range(heads)]
+        spread = jnp.zeros((batch * slots, HD), jnp.float32)
+        for h, (_, top, total) in enumerate(weighed):
             spread = jnp.where(lanes == h, top + jnp.log(total), spread)
-        stat_send[d] = jnp.transpose(spread)[:8]
-        stat_copy(d).start()
-        part_copy(d).start()
+        for i in range(batch):
+            stat_send[first + i] = jnp.transpose(spread[i * slots : (i + 1) * slots])[:8]
+        inverse = [1.0 / total for _, _, total in weighed]
+        if pair == 2:
+
+            @pl.when(first == 0)
+            def _():
+                kv_copy(1).wait_recv()
+
+        values = kv[1].reshape(pair * tokens, width)
+        for h, (weights, _, _) in enumerate(weighed):
+            at = slice(h * HD, (h + 1) * HD)
+            blend = (blend_of(weights, values, h) * inverse[h]).astype(jnp.bfloat16)
+            for i in range(batch):
+                part_send[first + i, :, at] = blend[i * slots : (i + 1) * slots]
+        for i in range(batch):
+
+            @pl.when(first + i != group)
+            def _():
+                stat_copy(first + i).start()
+                part_copy(first + i).start()
+
         return carry
 
-    loop(1, groups, answer, 0)
-    state = merge(state, attend(query[...], keys, values))
-
-    def gather(d, carry):
-        source = lax.rem(group + groups - d, groups)
-        arrived(stat_recv, stat_recv_sem, source)
-        arrived(part_recv, part_recv_sem, source)
-        spread = jnp.transpose(stat_recv[source])
-        other = [
+    loop(0, groups // batch, answer, 0)
+
+    def taken(buffer, stats, source):
+        spread = jnp.transpose(stats[source])
+        return [
             (
-                part_recv[source, :, h * HD : (h + 1) * HD].astype(jnp.float32),
+                buffer[source, :, h * HD : (h + 1) * HD].astype(jnp.float32),
                 spread[:, h : h + 1],
                 jnp.ones((slots, 1), jnp.float32),
             )
             for h in range(heads)
         ]
-        return merge(carry, other)
+
+    state = merge(state, taken(part_send, stat_send, group))
+
+    def gather(d, carry):
+        source = lax.rem(group + groups - d, groups)
+        arrived(stat_recv, stat_recv_sem, source)
+        arrived(part_recv, part_recv_sem, source)
+        return merge(carry, taken(part_recv, stat_recv, source))
 
     state = loop(1, groups, gather, state)
     attended = jnp.concatenate(
@@ -325,7 +377,7 @@
             device_id_type=MESH,
         )
 
-    for d in range(1, n_head):
+    for d in reversed(range(1, n_head)):
         w_out_in[d].wait()
         cols_send[d] = jnp.dot(attended, w_out[d], preferred_element_type=jnp.float32).astype(
             jnp.bfloat16
@@ -336,6 +388,8 @@
     residual = hidden[...].astype(jnp.float32) + jnp.dot(
         attended, w_out[0], preferred_element_type=jnp.float32
     )
+    for copy in last_in:
+        copy.wait()
     for d in range(1, n_head):
         cols_copy(d).wait_recv()
         residual = residual + cols_recv[d].astype(jnp.float32)
@@ -358,7 +412,7 @@
             device_id_type=MESH,
         )
 
-    for d in range(1, n_head):
+    for d in reversed(range(1, n_head)):
         sums_copy(d).start()
     for d in range(1, n_head):
         source = head_peer(d)
@@ -383,9 +437,16 @@
         fresh = fresh + sums[i, 0:slots, 0:channels] + away * column
         offset = offset + sums[i, slots + 1 : slots + 2, 0:channels]
     fresh = fresh * lax.rsqrt(squares / model + EPS) + offset
-    chosen[...] = jnp.transpose(
-        jnp.dot(one_hot, fresh, precision=HIGH, preferred_element_type=jnp.float32)
-    )
+    parts, rest = [], fresh
+    for _ in range(3):
+        parts.append(rest.astype(jnp.bfloat16))
+        rest = rest - parts[-1].astype(jnp.float32)
+    mask = one_hot.astype(jnp.bfloat16)
+    chosen = [jnp.dot(mask, part, preferred_element_type=jnp.float32) for part in parts]
+    chosen = chosen[0] + (chosen[1] + chosen[2])
+    chosen = jnp.transpose(jnp.where(replaced, chosen, jnp.transpose(cached_velocity[...])))
+    result[0] = chosen
+    result[1] = latent[...] + step_size[...] * chosen
 
     if pair == 2:
         kv_copy(0).wait_send()
@@ -393,8 +454,8 @@
 
     def drain(d, carry):
         q_copy(d).wait_send()
-        part_copy(d).wait_send()
-        stat_copy(d).wait_send()
+        part_copy(group_peer(d)).wait_send()
+        stat_copy(group_peer(d)).wait_send()
         return carry
 
     loop(1, groups, drain, 0)
@@ -431,24 +492,23 @@
     hbm = pl.BlockSpec(memory_space=pltpu.HBM)
     dma = pltpu.SemaphoreType.DMA
     flops = 2 * slots * (2 * width * (n_seq * tokens + text_kv.shape[1]) + width * share * n_head)
-    chosen, renewed = pl.pallas_call(
+    result = pl.pallas_call(
         functools.partial(kernel, n_seq, n_head, pair),
-        out_shape=(
-            jax.ShapeDtypeStruct((channels, tokens), jnp.float32),
-            jax.ShapeDtypeStruct((channels, tokens), jnp.float32),
-        ),
-        in_specs=[hbm] * 11,
-        out_specs=(vmem, vmem),
+        out_shape=jax.ShapeDtypeStruct((2, channels, tokens), jnp.float32),
+        in_specs=[hbm] * 14,
+        out_specs=vmem,
         scratch_shapes=[
-            pltpu.VMEM(query.shape, jnp.bfloat16),
             pltpu.VMEM(new_kv.shape, jnp.bfloat16),
             pltpu.VMEM(cache_kv.shape, jnp.bfloat16),
             pltpu.VMEM((1, slots), jnp.int32),
-            pltpu.SMEM((1,), jnp.int32),
+            pltpu.VMEM((1, 1), jnp.int32),
             pltpu.VMEM(hidden.shape, jnp.bfloat16),
             pltpu.VMEM((share // 128, 128), jnp.float32),
             pltpu.VMEM((share // 128, 128), jnp.float32),
             pltpu.VMEM((channels, share), jnp.float32),
+            pltpu.VMEM((channels, tokens), jnp.float32),
+            pltpu.VMEM((channels, tokens), jnp.float32),
+            pltpu.VMEM((1, 1), jnp.float32),
             pltpu.VMEM((groups, slots, width), jnp.bfloat16),
             pltpu.VMEM((2, pair, tokens, width), jnp.bfloat16),
             pltpu.VMEM(text_kv.shape, jnp.bfloat16),
@@ -460,7 +520,7 @@
             pltpu.VMEM((n_head, slots, share), jnp.bfloat16),
             pltpu.VMEM((n_head, slots, share), jnp.bfloat16),
             pltpu.VMEM((n_head, slots + 8, 128), jnp.float32),
-            dma((10 + n_head,)),
+            dma((13 + n_head,)),
             dma((2,)),
             dma((2,)),
             dma((groups,)),
@@ -486,16 +546,17 @@
         cache_kv,
         text_kv,
         active.reshape(1, slots),
-        counts,
+        counts.reshape(1, 1),
         hidden,
         w_out,
         mod_shift.reshape(share // 128, 128),
         mod_scale.reshape(share // 128, 128),
         w_final.T,
+        latent.T,
+        cached_velocity.T,
+        step_size.reshape(1, 1),
     )
-    velocity = jnp.where(renewed > 0.5, chosen, cached_velocity.T)
-    latent_next = latent.T + step_size[0] * velocity
-    return (velocity.T, latent_next.T)
+    return (result[0].T, result[1].T)
 
 
 def solution(mesh):

time: 30.8 us -> 29.6 us (0.961)
  other arithmetic: 1.41 us -> 0 us
  local copies, waits for them, and re-layouts: 0.01 us -> 1.4 us
  Pallas kernels: 27.1 us -> 26 us
    transpose x1 -> x0, other arithmetic: 1.41 us -> none  [on_device(): return (velocity.T, latent_next.T)]
    transpose x0 -> x1, local copies, waits for them, and re-layouts: none -> 1.4 us  [on_device(): return (result[0].T, result[1].T)]
    pallas_call x1, Pallas kernels: 27.1 us -> 26 us  [on_device(): pl.pallas_call(functools.partial(kernel, n_seq, n_head, pair), out_shape=...]
where the time goes in v3:
time: 29.6 us; the launch traced here: 29.4 us
  Pallas kernels  26 us (88%)
  between operations  1.93 us (7%)
  local copies, waits for them, and re-layouts  1.4 us (5%)
    pallas_call x1, Pallas kernels, on_device(): pl.pallas_call(functools.partial(kernel, n_seq, n_head, pair), out_shape=...  26 us
    transpose x1, local copies, waits for them, and re-layouts, on_device(): return (result[0].T, result[1].T)  1.4 us

profile of v3, /device:TPU:0, one launch (start us, length us, event | category | flops | bytes accessed | tf_op | source)
XLA Modules:
  0.0 29.4 jit_solution(2765403283190774778)
XLA Ops:
  1.9 26.0 %shard_map.149 = f32[2,64,128]{2,1,0:T(8,128)} custom-call(bf16[48,384]{1,0:T(8,128)(2,1)} %query_hbm.1, bf16[2,48,384]{2,1,0:T(8,128)(2,1)} %new_kv_hbm.1, bf16[2,128,384]{2,1,0:T(8,128)(2,1)} %cache_kv_hbm.1, bf16[2,512,384]{2,1,0:T(8,128)(2,1)} %text_hbm.1, s32[1,48]{1,0:T(1,128)} %bitcast.23, s32[1,1]{1,0:T(1,128)} %bitcast.16.counts_hbm, ...), custom_call_target="tpu_custom_call" | custom-call | flops 226492416 | bytes 2359296 | tf_op jit(solution)/shard_map/pallas_call | solution.py:495
  28.0 1.4 %slice_bitcast_fusion = (f32[128,64]{0,1:T(8,128)}, f32[128,64]{0,1:T(8,128)}) fusion(f32[2,64,128]{2,1,0:T(8,128)} %shard_map.149), kind=kLoop, calls=%fused_computation | loop fusion | bytes 131072 | tf_op jit(solution)/shard_map/transpose | solution.py:559

commit v4 on v3

--- a/solution.py
+++ b/solution.py
@@ -112,6 +112,9 @@
     for d in range(1, n_head):
         pl.semaphore_signal(barrier, inc=1, device_id=(seq, head_peer(d)), device_id_type=MESH)
 
+    def cut(h):
+        return slice(h * HD, (h + 1) * HD)
+
     local = []
 
     def fetch(source, target):
@@ -121,7 +124,7 @@
         return copy
 
     first_in = [
-        fetch(query_hbm, q_all.at[group]),
+        *[fetch(query_hbm.at[:, cut(h)], q_all.at[h, group]) for h in range(heads)],
         fetch(active_hbm, active),
         fetch(counts_hbm, counts),
         fetch(new_kv_hbm, new_kv),
@@ -158,75 +161,65 @@
             one_hot.astype(jnp.bfloat16), new_kv[which], preferred_element_type=jnp.float32
         )
         own = cache_kv[which].astype(jnp.float32)
-        kv[which, 0] = jnp.where(replaced, placed, own).astype(jnp.bfloat16)
+        merged = jnp.where(replaced, placed, own).astype(jnp.bfloat16)
+        for h in range(heads):
+            kv[h, 0, which] = merged[:, cut(h)]
 
     place_rows(0)
     place_rows(1)
     pl.semaphore_wait(barrier, groups - 1 + pair - 1 + n_head - 1)
 
-    def q_copy(d):
+    def q_copy(h, d):
         return pltpu.make_async_remote_copy(
-            src_ref=q_all.at[group],
-            dst_ref=q_all.at[group],
-            send_sem=q_send_sem.at[d],
-            recv_sem=q_recv_sem.at[group],
+            src_ref=q_all.at[h, group],
+            dst_ref=q_all.at[h, group],
+            send_sem=q_send_sem.at[h, d],
+            recv_sem=q_recv_sem.at[h, group],
             device_id=(group_peer(d) * pair + place, head),
             device_id_type=MESH,
         )
 
-    def kv_copy(which):
+    def kv_copy(h):
         return pltpu.make_async_remote_copy(
-            src_ref=kv.at[which, 0],
-            dst_ref=kv.at[which, 1],
-            send_sem=kv_send_sem.at[which],
-            recv_sem=kv_recv_sem.at[which],
+            src_ref=kv.at[h, 0],
+            dst_ref=kv.at[h, 1],
+            send_sem=kv_send_sem.at[h],
+            recv_sem=kv_recv_sem.at[h],
             device_id=(partner, head),
             device_id_type=MESH,
         )
 
-    def start_q(d, carry):
-        q_copy(d).start()
-        return carry
-
-    if pair == 2:
-        kv_copy(0).start()
-    loop(1, groups, start_q, 0)
-    if pair == 2:
-        kv_copy(1).start()
-
-    def weigh(rows, keys, h):
-        at = slice(h * HD, (h + 1) * HD)
+    for h in range(heads):
+
+        def start_q(d, carry):
+            q_copy(h, d).start()
+            return carry
+
+        if pair == 2:
+            kv_copy(h).start()
+        loop(1, groups, start_q, 0)
+
+    def weigh(rows, keys):
         scores = lax.dot_general(
-            rows[:, at],
-            keys[:, at],
-            (((1,), (1,)), ((), ())),
-            preferred_element_type=jnp.float32,
+            rows, keys, (((1,), (1,)), ((), ())), preferred_element_type=jnp.float32
         ) * HD ** (-0.5)
         top = jnp.max(scores, axis=1, keepdims=True)
         weights = jnp.exp(scores - top)
         total = jnp.sum(weights, axis=1, keepdims=True)
         return weights.astype(jnp.bfloat16), top, total
 
-    def blend_of(weights, values, h):
-        return jnp.dot(
-            weights,
-            values[:, h * HD : (h + 1) * HD],
-            preferred_element_type=jnp.float32,
-        )
+    def blend_of(weights, values):
+        return jnp.dot(weights, values, preferred_element_type=jnp.float32)
 
     def merge(first, second):
-        result = []
-        for (blend_a, top_a, total_a), (blend_b, top_b, total_b) in zip(first, second):
-            top = jnp.maximum(top_a, top_b)
-            share_a, share_b = jnp.exp(top_a - top), jnp.exp(top_b - top)
-            result.append(
-                (
-                    blend_a * share_a + blend_b * share_b,
-                    top,
-                    total_a * share_a + total_b * share_b,
-                )
-            )
-        return result
+        (blend_a, top_a, total_a), (blend_b, top_b, total_b) = first, second
+        top = jnp.maximum(top_a, top_b)
+        share_a, share_b = jnp.exp(top_a - top), jnp.exp(top_b - top)
+        return (
+            blend_a * share_a + blend_b * share_b,
+            top,
+            total_a * share_a + total_b * share_b,
+        )
 
     for copy in norm_in:
         copy.wait()
@@ -259,113 +252,95 @@
     sums[head, slots : slots + 8, 0:channels] = final_dot(pairs)[:8]
     text_in.wait()
     state = []
-    own = q_all[group]
     for h in range(heads):
-        weights, top, total = weigh(own, text[0], h)
-        state.append((blend_of(weights, text[1], h), top, total))
-
-    def part_copy(to):
+        weights, top, total = weigh(q_all[h, group], text[0, :, cut(h)])
+        state.append((blend_of(weights, text[1, :, cut(h)]), top, total))
+
+    def part_copy(h, to):
         return pltpu.make_async_remote_copy(
-            src_ref=part_send.at[to],
-            dst_ref=part_recv.at[group],
-            send_sem=part_send_sem.at[to],
-            recv_sem=part_recv_sem.at[group],
+            src_ref=part_send.at[h, to],
+            dst_ref=part_recv.at[h, group],
+            send_sem=part_send_sem.at[h, to],
+            recv_sem=part_recv_sem.at[h, group],
             device_id=(to * pair + place, head),
             device_id_type=MESH,
         )
 
-    def stat_copy(to):
+    def stat_copy(h, to):
         return pltpu.make_async_remote_copy(
-            src_ref=stat_send.at[to],
-            dst_ref=stat_recv.at[group],
-            send_sem=stat_send_sem.at[to],
-            recv_sem=stat_recv_sem.at[group],
+            src_ref=stat_send.at[h, to],
+            dst_ref=stat_recv.at[h, group],
+            send_sem=stat_send_sem.at[h, to],
+            recv_sem=stat_recv_sem.at[h, group],
             device_id=(to * pair + place, head),
             device_id_type=MESH,
         )
 
-    def arrived(buffer, sems, source):
+    def arrived(buffer, sems, h, source):
         pltpu.make_async_remote_copy(
-            src_ref=buffer.at[source],
-            dst_ref=buffer.at[source],
-            send_sem=q_send_sem.at[0],
-            recv_sem=sems.at[source],
+            src_ref=buffer.at[h, source],
+            dst_ref=buffer.at[h, source],
+            send_sem=q_send_sem.at[h, 0],
+            recv_sem=sems.at[h, source],
             device_id=(source * pair + place, head),
             device_id_type=MESH,
         ).wait_recv()
 
     batch = min(groups, 4) if groups % 4 == 0 or groups < 4 else 1
-    lanes = lax.broadcasted_iota(jnp.int32, (batch * slots, HD), 1)
-
-    def answer(step, carry):
-        first = step * batch
-        for i in range(batch):
-
-            @pl.when(first + i != group)
-            def _():
-                arrived(q_all, q_recv_sem, first + i)
-
+
+    for h in range(heads):
         if pair == 2:
-
-            @pl.when(first == 0)
-            def _():
-                kv_copy(0).wait_recv()
-
-        keys = kv[0].reshape(pair * tokens, width)
-        rows = q_all[pl.ds(first, batch)].reshape(batch * slots, width)
-        weighed = [weigh(rows, keys, h) for h in range(heads)]
-        spread = jnp.zeros((batch * slots, HD), jnp.float32)
-        for h, (_, top, total) in enumerate(weighed):
-            spread = jnp.where(lanes == h, top + jnp.log(total), spread)
-        for i in range(batch):
-            stat_send[first + i] = jnp.transpose(spread[i * slots : (i + 1) * slots])[:8]
-        inverse = [1.0 / total for _, _, total in weighed]
-        if pair == 2:
-
-            @pl.when(first == 0)
-            def _():
-                kv_copy(1).wait_recv()
-
-        values = kv[1].reshape(pair * tokens, width)
-        for h, (weights, _, _) in enumerate(weighed):
-            at = slice(h * HD, (h + 1) * HD)
-            blend = (blend_of(weights, values, h) * inverse[h]).astype(jnp.bfloat16)
+            kv_copy(h).wait_recv()
+
+        def answer(step, carry):
+            first = step * batch
             for i in range(batch):
-                part_send[first + i, :, at] = blend[i * slots : (i + 1) * slots]
-        for i in range(batch):
-
-            @pl.when(first + i != group)
-            def _():
-                stat_copy(first + i).start()
-                part_copy(first + i).start()
-
-        return carry
-
-    loop(0, groups // batch, answer, 0)
-
-    def taken(buffer, stats, source):
-        spread = jnp.transpose(stats[source])
-        return [
-            (
-                buffer[source, :, h * HD : (h + 1) * HD].astype(jnp.float32),
-                spread[:, h : h + 1],
-                jnp.ones((slots, 1), jnp.float32),
-            )
-            for h in range(heads)
-        ]
-
-    state = merge(state, taken(part_send, stat_send, group))
-
-    def gather(d, carry):
-        source = lax.rem(group + groups - d, groups)
-        arrived(stat_recv, stat_recv_sem, source)
-        arrived(part_recv, part_recv_sem, source)
-        return merge(carry, taken(part_recv, stat_recv, source))
-
-    state = loop(1, groups, gather, state)
-    attended = jnp.concatenate(
-        [(blend / total).astype(jnp.bfloat16) for blend, top, total in state], axis=1
-    )
+
+                @pl.when(first + i != group)
+                def _():
+                    arrived(q_all, q_recv_sem, h, first + i)
+
+            rows = q_all[h, pl.ds(first, batch)].reshape(batch * slots, HD)
+            weights, top, total = weigh(rows, kv[h, :, 0].reshape(pair * tokens, HD))
+            blend = blend_of(weights, kv[h, :, 1].reshape(pair * tokens, HD))
+            blend = (blend * (1.0 / total)).astype(jnp.bfloat16)
+            spread = jnp.broadcast_to(top + jnp.log(total), (batch * slots, HD))
+            for i in range(batch):
+                at = slice(i * slots, (i + 1) * slots)
+                part_send[h, first + i] = blend[at]
+                stat_send[h, first + i] = jnp.transpose(spread[at])[:8]
+            for i in range(batch):
+
+                @pl.when(first + i != group)
+                def _():
+                    stat_copy(h, first + i).start()
+                    part_copy(h, first + i).start()
+
+            return carry
+
+        loop(0, groups // batch, answer, 0)
+
+    def taken(buffer, stats, h, source):
+        spread = jnp.transpose(stats[h, source])
+        return (
+            buffer[h, source].astype(jnp.float32),
+            spread[:, :1],
+            jnp.ones((slots, 1), jnp.float32),
+        )
+
+    attended = []
+    for h in range(heads):
+
+        def gather(d, carry):
+            source = lax.rem(group + groups - d, groups)
+            arrived(stat_recv, stat_recv_sem, h, source)
+            arrived(part_recv, part_recv_sem, h, source)
+            return merge(carry, taken(part_recv, stat_recv, h, source))
+
+        merged = merge(state[h], taken(part_send, stat_send, h, group))
+        blend, _, total = loop(1, groups, gather, merged)
+        attended.append((blend / total).astype(jnp.bfloat16))
+    attended = jnp.concatenate(attended, axis=1)
 
     def cols_copy(d):
         return pltpu.make_async_remote_copy(
@@ -448,17 +423,17 @@
     result[0] = chosen
     result[1] = latent[...] + step_size[...] * chosen
 
-    if pair == 2:
-        kv_copy(0).wait_send()
-        kv_copy(1).wait_send()
-
-    def drain(d, carry):
-        q_copy(d).wait_send()
-        part_copy(group_peer(d)).wait_send()
-        stat_copy(group_peer(d)).wait_send()
-        return carry
-
-    loop(1, groups, drain, 0)
+    for h in range(heads):
+
+        def drain(d, carry):
+            q_copy(h, d).wait_send()
+            part_copy(h, group_peer(d)).wait_send()
+            stat_copy(h, group_peer(d)).wait_send()
+            return carry
+
+        if pair == 2:
+            kv_copy(h).wait_send()
+        loop(1, groups, drain, 0)
     for d in range(1, n_head):
         cols_copy(d).wait_send()
         sums_copy(d).wait_send()
@@ -488,6 +463,7 @@
     channels = w_final.shape[1]
     pair = 2 if n_seq % 2 == 0 else 1
     groups = n_seq // pair
+    heads = width // HD
     vmem = pl.BlockSpec(memory_space=pltpu.VMEM)
     hbm = pl.BlockSpec(memory_space=pltpu.HBM)
     dma = pltpu.SemaphoreType.DMA
@@ -509,26 +485,26 @@
             pltpu.VMEM((channels, tokens), jnp.float32),
             pltpu.VMEM((channels, tokens), jnp.float32),
             pltpu.VMEM((1, 1), jnp.float32),
-            pltpu.VMEM((groups, slots, width), jnp.bfloat16),
-            pltpu.VMEM((2, pair, tokens, width), jnp.bfloat16),
+            pltpu.VMEM((heads, groups, slots, HD), jnp.bfloat16),
+            pltpu.VMEM((heads, pair, 2, tokens, HD), jnp.bfloat16),
             pltpu.VMEM(text_kv.shape, jnp.bfloat16),
             pltpu.VMEM((n_head, width, share), jnp.bfloat16),
-            pltpu.VMEM((groups, slots, width), jnp.bfloat16),
-            pltpu.VMEM((groups, slots, width), jnp.bfloat16),
-            pltpu.VMEM((groups, 8, slots), jnp.float32),
-            pltpu.VMEM((groups, 8, slots), jnp.float32),
+            pltpu.VMEM((heads, groups, slots, HD), jnp.bfloat16),
+            pltpu.VMEM((heads, groups, slots, HD), jnp.bfloat16),
+            pltpu.VMEM((heads, groups, 8, slots), jnp.float32),
+            pltpu.VMEM((heads, groups, 8, slots), jnp.float32),
             pltpu.VMEM((n_head, slots, share), jnp.bfloat16),
             pltpu.VMEM((n_head, slots, share), jnp.bfloat16),
             pltpu.VMEM((n_head, slots + 8, 128), jnp.float32),
-            dma((13 + n_head,)),
-            dma((2,)),
-            dma((2,)),
-            dma((groups,)),
-            dma((groups,)),
-            dma((groups,)),
-            dma((groups,)),
-            dma((groups,)),
-            dma((groups,)),
+            dma((12 + heads + n_head,)),
+            dma((heads,)),
+            dma((heads,)),
+            dma((heads, groups)),
+            dma((heads, groups)),
+            dma((heads, groups)),
+            dma((heads, groups)),
+            dma((heads, groups)),
+            dma((heads, groups)),
             dma((n_head,)),
             dma((n_head,)),
             dma((n_head,)),

time: 29.6 us -> 29.6 us (level)
  no operation moved by 1% of the time
where the time goes in v4:
time: 29.6 us; the launch traced here: 29.4 us
  Pallas kernels  26 us (88%)
  between operations  1.93 us (7%)
  local copies, waits for them, and re-layouts  1.4 us (5%)
    pallas_call x1, Pallas kernels, on_device(): pl.pallas_call(functools.partial(kernel, n_seq, n_head, pair), out_shape=...  26 us
    transpose x1, local copies, waits for them, and re-layouts, on_device(): return (result[0].T, result[1].T)  1.4 us

profile of v4, /device:TPU:0, one launch (start us, length us, event | category | flops | bytes accessed | tf_op | source)
XLA Modules:
  0.0 29.4 jit_solution(10793081747635671315)
XLA Ops:
  1.9 26.0 %shard_map.149 = f32[2,64,128]{2,1,0:T(8,128)} custom-call(bf16[48,384]{1,0:T(8,128)(2,1)} %query_hbm.1, bf16[2,48,384]{2,1,0:T(8,128)(2,1)} %new_kv_hbm.1, bf16[2,128,384]{2,1,0:T(8,128)(2,1)} %cache_kv_hbm.1, bf16[2,512,384]{2,1,0:T(8,128)(2,1)} %text_hbm.1, s32[1,48]{1,0:T(1,128)} %bitcast.23, s32[1,1]{1,0:T(1,128)} %bitcast.16.counts_hbm, ...), custom_call_target="tpu_custom_call" | custom-call | flops 226492416 | bytes 2359296 | tf_op jit(solution)/shard_map/pallas_call | solution.py:471
  28.0 1.4 %slice_bitcast_fusion = (f32[128,64]{0,1:T(8,128)}, f32[128,64]{0,1:T(8,128)}) fusion(f32[2,64,128]{2,1,0:T(8,128)} %shard_map.149), kind=kLoop, calls=%fused_computation | loop fusion | bytes 131072 | tf_op jit(solution)/shard_map/transpose | solution.py:535

commit v5 on v4

--- a/solution.py
+++ b/solution.py
@@ -221,41 +221,6 @@
             total_a * share_a + total_b * share_b,
         )
 
-    for copy in norm_in:
-        copy.wait()
-
-    def as_row(ref):
-        return jnp.concatenate([ref[i : i + 1, :] for i in range(ref.shape[0])], axis=1)
-
-    lifted = 1.0 + as_row(mod_scale)
-
-    def split(x):
-        top = x.astype(jnp.bfloat16)
-        return top, (x - top.astype(jnp.float32)).astype(jnp.bfloat16)
-
-    final_top, final_rest = split(w_final[...])
-
-    def final_dot(rows):
-        count = rows.shape[0]
-        top, rest = split(rows)
-
-        def times(left, right):
-            return lax.dot_general(
-                left, right, (((1,), (1,)), ((), ())), preferred_element_type=jnp.float32
-            )
-
-        both = times(jnp.concatenate([top, rest], axis=0), final_top)
-        return both[:count] + (both[count:] + times(top, final_rest))
-
-    rows8 = lax.broadcasted_iota(jnp.int32, (16, share), 0)
-    pairs = jnp.where(rows8 == 0, lifted, jnp.where(rows8 == 1, as_row(mod_shift), 0.0))
-    sums[head, slots : slots + 8, 0:channels] = final_dot(pairs)[:8]
-    text_in.wait()
-    state = []
-    for h in range(heads):
-        weights, top, total = weigh(q_all[h, group], text[0, :, cut(h)])
-        state.append((blend_of(weights, text[1, :, cut(h)]), top, total))
-
     def part_copy(h, to):
         return pltpu.make_async_remote_copy(
             src_ref=part_send.at[h, to],
@@ -319,6 +284,41 @@
             return carry
 
         loop(0, groups // batch, answer, 0)
+
+    for copy in norm_in:
+        copy.wait()
+
+    def as_row(ref):
+        return jnp.concatenate([ref[i : i + 1, :] for i in range(ref.shape[0])], axis=1)
+
+    lifted = 1.0 + as_row(mod_scale)
+
+    def split(x):
+        top = x.astype(jnp.bfloat16)
+        return top, (x - top.astype(jnp.float32)).astype(jnp.bfloat16)
+
+    final_top, final_rest = split(w_final[...])
+
+    def final_dot(rows):
+        count = rows.shape[0]
+        top, rest = split(rows)
+
+        def times(left, right):
+            return lax.dot_general(
+                left, right, (((1,), (1,)), ((), ())), preferred_element_type=jnp.float32
+            )
+
+        both = times(jnp.concatenate([top, rest], axis=0), final_top)
+        return both[:count] + (both[count:] + times(top, final_rest))
+
+    rows8 = lax.broadcasted_iota(jnp.int32, (16, share), 0)
+    pairs = jnp.where(rows8 == 0, lifted, jnp.where(rows8 == 1, as_row(mod_shift), 0.0))
+    sums[head, slots : slots + 8, 0:channels] = final_dot(pairs)[:8]
+    text_in.wait()
+    state = []
+    for h in range(heads):
+        weights, top, total = weigh(q_all[h, group], text[0, :, cut(h)])
+        state.append((blend_of(weights, text[1, :, cut(h)]), top, total))
 
     def taken(buffer, stats, h, source):
         spread = jnp.transpose(stats[h, source])

time: 29.6 us -> 29.6 us (level)
  no operation moved by 1% of the time
where the time goes in v5:
time: 29.6 us; the launch traced here: 29.3 us
  Pallas kernels  26 us (88%)
  between operations  1.93 us (7%)
  local copies, waits for them, and re-layouts  1.4 us (5%)
    pallas_call x1, Pallas kernels, on_device(): pl.pallas_call(functools.partial(kernel, n_seq, n_head, pair), out_shape=...  26 us
    transpose x1, local copies, waits for them, and re-layouts, on_device(): return (result[0].T, result[1].T)  1.4 us

profile of v5, /device:TPU:0, one launch (start us, length us, event | category | flops | bytes accessed | tf_op | source)
XLA Modules:
  0.0 29.3 jit_solution(3291315890067846851)
XLA Ops:
  1.9 26.0 %shard_map.149 = f32[2,64,128]{2,1,0:T(8,128)} custom-call(bf16[48,384]{1,0:T(8,128)(2,1)} %query_hbm.1, bf16[2,48,384]{2,1,0:T(8,128)(2,1)} %new_kv_hbm.1, bf16[2,128,384]{2,1,0:T(8,128)(2,1)} %cache_kv_hbm.1, bf16[2,512,384]{2,1,0:T(8,128)(2,1)} %text_hbm.1, s32[1,48]{1,0:T(1,128)} %bitcast.23, s32[1,1]{1,0:T(1,128)} %bitcast.16.counts_hbm, ...), custom_call_target="tpu_custom_call" | custom-call | flops 226492416 | bytes 2359296 | tf_op jit(solution)/shard_map/pallas_call | solution.py:471
  27.9 1.4 %slice_bitcast_fusion = (f32[128,64]{0,1:T(8,128)}, f32[128,64]{0,1:T(8,128)}) fusion(f32[2,64,128]{2,1,0:T(8,128)} %shard_map.149), kind=kLoop, calls=%fused_computation | loop fusion | bytes 131072 | tf_op jit(solution)/shard_map/transpose | solution.py:535
